TPU v7x, 256 devices: a whole 4x4x8 slice. The times are simulated.
256 devices in a mesh: surf: 128 (over z, y, x), wall: 2 (over core).
Axes of the slice: x: 4, y: 4, z: 8, core: 2. Of those that a mesh axis runs over, the one named last changes fastest.
Arguments:
- rhs: float32 [2, 64, 16384], P('wall', None, 'surf'), may hold values from -6 to 6
- prev_solution: float32 [2, 64, 16384], P('wall', None, 'surf'), may hold values from -6 to 6
- lower: float32 [2, 64, 64, 16384], P('wall', None, None, 'surf'), as said below
- pivot_inv: float32 [2, 64, 64, 16384], P('wall', None, None, 'surf'), as said below
- upper_back: float32 [2, 64, 64, 16384], P('wall', None, None, 'surf'), as said below
- coupling: float32 [4, 2, 64, 16384], P(None, 'wall', None, 'surf'), may hold values from -0.5 to 0.5
- neighbours: int32 [4, 16384], P(None, 'surf'), may hold values from 0 to 16383, as said below
- counts: int32 [16384], P('surf'), may hold values from 1 to 2
- colour: int32 [16384], P('surf'), may hold values 0 or 1
Outputs:
- new_solution: float32 [2, 64, 16384], P('wall', None, 'surf')
Inputs may be any that keep to these rules, and one draw needn't show every extreme that they name: `neighbours`: each neighbour line is held by the same index of surf as the line, or by the index one below or one above it, cyclically. `lower`: dominant diagonal; the forward recurrence neither grows nor vanishes over a line. `pivot_inv`: dominant diagonal. `upper_back`: dominant diagonal; the backward recurrence neither grows nor vanishes over a line.
All inputs are finite; a program needn't handle non-finite values. No bound on the sum of `colour` on one device may be relied on, other than what follows from the above.
Results may differ from a plain program's by a relative error of at most 0.0001.
Values sent between devices are 32-bit elements; how exact they have to be, the bound alone decides.
A program may use at most 64 MiB of HBM per device.

v0:
```python
import jax
import jax.numpy as jnp
from jax import lax
from jax.sharding import PartitionSpec as P


def padded(array, sides, width):
    for axis, dim in sides:
        peers, length = (lax.axis_size(axis), array.shape[dim])
        up = [(i, (i + 1) % peers) for i in range(peers)]
        down = [(j, i) for i, j in up]
        last = lax.slice_in_dim(array, length - width, length, axis=dim)
        first = lax.slice_in_dim(array, 0, width, axis=dim)
        before = lax.ppermute(last, axis, up)
        after = lax.ppermute(first, axis, down)
        array = jnp.concatenate([before, array, after], axis=dim)
    return array


def from_behind(value, axis, steps):
    count = lax.axis_size(axis)
    first, last = (max(0, -steps), min(count, count - steps))
    return lax.ppermute(value, axis, [(source, source + steps) for source in range(first, last)])


def matvec(mat, vec):
    return jnp.einsum("abl,bl->al", mat, vec, precision=lax.Precision.HIGHEST)


def shards(rhs, prev_solution, lower, pivot_inv, upper_back, coupling, neighbours, counts, colour):
    seg_count = rhs.shape[0]
    block = rhs.shape[1]
    line_count = rhs.shape[2]
    wall_pos = lax.axis_index("wall")
    row_ids = wall_pos * seg_count + jnp.arange(seg_count, dtype=jnp.int32)
    active = (row_ids[:, None] < counts[None, :]).astype(jnp.float32)
    zeros = jnp.zeros((block, line_count), jnp.float32)
    forward_maps = [-active[0][None, None, :] * lower[0]]
    backward_maps = [None] * seg_count
    backward_maps[seg_count - 1] = -active[seg_count - 1][None, None, :] * upper_back[seg_count - 1]
    owners = neighbours // line_count
    surf_pos = lax.axis_index("surf")
    groups = lax.axis_size("surf")
    distance = (owners - surf_pos + groups) % groups
    offsets = jnp.where(distance == groups - 1, -1, distance)
    positions = (offsets + 1) * line_count + neighbours % line_count

    def source_of(field):
        gathered = padded(field, (("surf", 2),), line_count)
        total = rhs
        for face in range(coupling.shape[0]):
            total = total - coupling[face] * jnp.take(gathered, positions[face], axis=2)
        return total

    def line_solve(source):
        carry = zeros
        row = 0
        carry = active[row][None, :] * (source[row] - matvec(lower[row], carry))
        partial_fwd = [carry]
        incoming = zeros
        outgoing = partial_fwd[-1] + matvec(forward_maps[-1], incoming)
        incoming = from_behind(outgoing, "wall", 1)
        forward_vals = [partial_fwd[0] + matvec(forward_maps[0], incoming)]
        partial_back = [None] * seg_count
        carry = zeros
        row = 0
        carry = active[row][None, :] * (
            matvec(pivot_inv[row], forward_vals[row]) - matvec(upper_back[row], carry)
        )
        partial_back[row] = carry
        arriving = zeros
        leaving = partial_back[0] + matvec(backward_maps[0], arriving)
        arriving = from_behind(leaving, "wall", -1)
        return jnp.stack([partial_back[0] + matvec(backward_maps[0], arriving)], axis=0)

    first = line_solve(source_of(prev_solution))
    current = jnp.where((colour == 0)[None, None, :], first, prev_solution)
    second = line_solve(source_of(current))
    return jnp.where((colour == 1)[None, None, :], second, current)


def solution(mesh):
    placed = (
        P("wall", None, "surf"),
        P("wall", None, "surf"),
        P("wall", None, None, "surf"),
        P("wall", None, None, "surf"),
        P("wall", None, None, "surf"),
        P(None, "wall", None, "surf"),
        P(None, "surf"),
        P("surf"),
        P("surf"),
    )
    return jax.shard_map(
        shards, mesh=mesh, in_specs=placed, out_specs=P("wall", None, "surf"), check_vma=False
    )
```

profile of v0, /device:TPU:1, one launch (start us, length us, event | category | flops | bytes accessed | tf_op | source)
XLA Modules:
  0.0 90.5 jit_solution(15465201979521710214)
XLA Ops:
  0.0 0.8 copy.11
  0.9 2.1 %collective-permute-start = (f32[1,64,128]{1,2,0:T(8,128)S(1)}, f32[1,64,128]{1,2,0:T(8,128)S(1)}, u32[]{:S(2)}, u32[]{:S(2)}) collective-permute-start(f32[1,64,128]{1,2,0:T(8,128)S(1)} %copy.11), channel_id=1, source_target_pairs={{0,2},{2,4},{4,6},{6,8},{8,10},{10,12},{12,14},{14,16},{16,18},{18... | collective-permute-start | bytes 98312 | tf_op jit(solution)/shard_map/ppermute | solution.py:14
  3.0 9.1 %collective-permute-start.1 = (f32[1,64,128]{1,2,0:T(8,128)S(1)}, f32[1,64,128]{1,2,0:T(8,128)S(1)}, u32[]{:S(2)}, u32[]{:S(2)}) collective-permute-start(f32[1,64,128]{1,2,0:T(8,128)S(1)} %copy.11), channel_id=1, source_target_pairs={{2,0},{4,2},{6,4},{8,6},{10,8},{12,10},{14,12},{16,14},{18,16},{20... | collective-permute-start | bytes 98312 | tf_op jit(solution)/shard_map/ppermute | solution.py:15
  12.1 0.7 fusion.27
  12.8 0.8 fusion.34
  13.6 0.7 fusion.33
  14.3 5.3 %multiply_reduce_fusion.1 = (f32[128,64]{0,1:T(8,128)S(1)}, f32[64,64,128]{2,1,0:T(8,128)}, f32[128,64]{0,1:T(8,128)S(1)}, f32[128,64]{0,1:T(8,128)S(1)}, f32[128,64]{0,1:T(8,128)S(1)}, /*index=5*/f32[64,64,128]{2,1,0:T(8,128)S(1)}) fusion(f32[1,64,64,128]{3,2,1,0:T(8,128)} %param.13, f32[128]{0:T(128)S(1)} %get-tuple-element.22, f32[1,64,64,128]{3,2,1,0:T(8,128)} %param.15), kind=kLoop, calls=%fused_computation.15 | loop fusion | flops 5210112 | bytes 8520192
  19.6 0.1 copy.27
  19.7 0.1 copy.34
  19.8 0.1 copy.64
  19.9 0.1 copy.65
  20.0 0.1 copy.66
  20.1 0.1 copy.67
  20.2 0.1 copy.19
  20.3 0.6 gather_fusion.2
  21.0 0.6 gather_fusion.3
  21.6 0.6 gather_fusion
  22.3 0.6 gather_fusion.1
  22.9 0.2 bitcast_add_fusion.1
  23.1 1.5 %collective-permute-start.2 = (f32[64,128]{0,1:T(8,128)S(1)}, f32[64,128]{0,1:T(8,128)S(1)}, u32[]{:S(2)}, u32[]{:S(2)}) collective-permute-start(f32[64,128]{0,1:T(8,128)S(1)} %get-tuple-element.8), channel_id=1, source_target_pairs={{0,1},{2,3},{4,5},{6,7},{8,9},{10,11},{12,13},{14,15},{16,17},{18,... | collective-permute-start | bytes 98312 | tf_op jit(solution)/shard_map/ppermute | solution.py:23
  24.5 5.6 %copy.36 = f32[64,64,128]{0,1,2:T(8,128)} copy(f32[64,64,128]{2,1,0:T(8,128)} %get-tuple-element.11) | data formatting | bytes 4194304 | tf_op jit(solution)/shard_map/mul | solution.py:38
  30.2 5.6 %copy.39 = f32[64,64,128]{0,1,2:T(8,128)} copy(f32[64,64,128]{2,1,0:T(8,128)} %bitcast.243) | data formatting | bytes 4194304 | tf_op jit(solution)/shard_map/squeeze | solution.py:68
  35.8 0.1 copy.47
  35.9 0.1 copy.54
  36.0 5.4 %fusion.35 = f32[128,1,64]{2,1,0:T(1,128)S(1)} fusion(f32[64,128,1]{0,2,1:T(1,128)S(1)} %bitcast.254, f32[64,64,128]{0,1,2:T(8,128)} %copy.36), kind=kOutput, calls=%fused_computation.90 | convolution fusion | flops 6291456 | bytes 2162688 | tf_op jit(solution)/shard_map/abl,bl->al/dot_general | solution.py:27
  41.5 3.7 %fusion.36 = f32[128,1,64]{2,1,0:T(1,128)S(1)} fusion(f32[64,128,1]{0,2,1:T(1,128)S(1)} %bitcast.253, f32[64,64,128]{0,1,2:T(8,128)S(1)} %copy-done), kind=kOutput, calls=%fused_computation.91 | convolution fusion | flops 6291456 | bytes 2162688 | tf_op jit(solution)/shard_map/abl,bl->al/dot_general | solution.py:27
  45.2 0.1 add_bitcast_fusion.1
  45.2 3.0 %collective-permute-start.3 = (f32[64,128]{0,1:T(8,128)S(1)}, f32[64,128]{0,1:T(8,128)S(1)}, u32[]{:S(2)}, u32[]{:S(2)}) collective-permute-start(f32[64,128]{0,1:T(8,128)S(1)} %add_bitcast_fusion.1), channel_id=1, source_target_pairs={{1,0},{3,2},{5,4},{7,6},{9,8},{11,10},{13,12},{15,14},{17,16},{19,... | collective-permute-start | bytes 98312 | tf_op jit(solution)/shard_map/ppermute | solution.py:23
  48.3 4.6 %copy.56 = f32[64,64,128]{0,1,2:T(8,128)} copy(f32[64,64,128]{2,1,0:T(8,128)S(1)} %get-tuple-element.38) | data formatting | bytes 4194304 | tf_op jit(solution)/shard_map/mul | solution.py:40
  52.9 5.3 %fusion.37 = f32[128,1,64]{2,1,0:T(1,128)S(1)} fusion(f32[64,128,1]{0,2,1:T(1,128)S(1)} %bitcast.255, f32[64,64,128]{0,1,2:T(8,128)} %copy.56), kind=kOutput, calls=%fused_computation.92 | convolution fusion | flops 6291456 | bytes 2162688 | tf_op jit(solution)/shard_map/abl,bl->al/dot_general | solution.py:27
  58.2 0.1 bitcast_select_fusion.5
  58.4 6.9 %collective-permute-start.5 = (f32[1,64,128]{1,2,0:T(8,128)S(1)}, f32[1,64,128]{1,2,0:T(8,128)S(1)}, u32[]{:S(2)}, u32[]{:S(2)}) collective-permute-start(f32[1,64,128]{1,2,0:T(8,128)S(1)} %bitcast_select_fusion.5), channel_id=1, source_target_pairs={{2,0},{4,2},{6,4},{8,6},{10,8},{12,10},{14,12},{16,14},{18,16},{20... | collective-permute-start | bytes 98312 | tf_op jit(solution)/shard_map/ppermute | solution.py:15
  65.3 2.3 %collective-permute-done.4 = f32[1,64,128]{1,2,0:T(8,128)S(1)} collective-permute-done((f32[1,64,128]{1,2,0:T(8,128)S(1)}, f32[1,64,128]{1,2,0:T(8,128)S(1)}, u32[]{:S(2)}, u32[]{:S(2)}) %collective-permute-start.4) | collective-permute-done | bytes 32800 | tf_op jit(solution)/shard_map/ppermute | solution.py:14
  67.6 0.6 gather_fusion.4
  68.3 0.6 gather_fusion.5
  68.9 0.6 gather_fusion.6
  69.6 0.6 gather_fusion.7
  70.2 0.2 bitcast_add_fusion
  70.4 1.6 %collective-permute-start.6 = (f32[64,128]{0,1:T(8,128)S(1)}, f32[64,128]{0,1:T(8,128)S(1)}, u32[]{:S(2)}, u32[]{:S(2)}) collective-permute-start(f32[64,128]{0,1:T(8,128)S(1)} %get-tuple-element.6), channel_id=1, source_target_pairs={{0,1},{2,3},{4,5},{6,7},{8,9},{10,11},{12,13},{14,15},{16,17},{18,... | collective-permute-start | bytes 98312 | tf_op jit(solution)/shard_map/ppermute | solution.py:23
  71.9 1.8 %collective-permute-done.6 = f32[64,128]{0,1:T(8,128)S(1)} collective-permute-done((f32[64,128]{0,1:T(8,128)S(1)}, f32[64,128]{0,1:T(8,128)S(1)}, u32[]{:S(2)}, u32[]{:S(2)}) %collective-permute-start.6) | collective-permute-done | bytes 32800 | tf_op jit(solution)/shard_map/ppermute | solution.py:23
  73.8 5.4 %fusion.38 = f32[128,1,64]{2,1,0:T(1,128)S(1)} fusion(f32[64,128,1]{0,2,1:T(1,128)S(1)} %bitcast.256, f32[64,64,128]{0,1,2:T(8,128)} %copy.36), kind=kOutput, calls=%fused_computation.93 | convolution fusion | flops 6291456 | bytes 2162688 | tf_op jit(solution)/shard_map/abl,bl->al/dot_general | solution.py:27
  79.2 3.7 %fusion.39 = f32[128,1,64]{2,1,0:T(1,128)S(1)} fusion(f32[64,128,1]{0,2,1:T(1,128)S(1)} %bitcast.252, f32[64,64,128]{0,1,2:T(8,128)S(1)} %copy-done.1), kind=kOutput, calls=%fused_computation.94 | convolution fusion | flops 6291456 | bytes 2162688 | tf_op jit(solution)/shard_map/abl,bl->al/dot_general | solution.py:27
  82.9 0.1 add_bitcast_fusion
  83.0 2.1 %collective-permute-start.7 = (f32[64,128]{0,1:T(8,128)S(1)}, f32[64,128]{0,1:T(8,128)S(1)}, u32[]{:S(2)}, u32[]{:S(2)}) collective-permute-start(f32[64,128]{0,1:T(8,128)S(1)} %add_bitcast_fusion), channel_id=1, source_target_pairs={{1,0},{3,2},{5,4},{7,6},{9,8},{11,10},{13,12},{15,14},{17,16},{19,... | collective-permute-start | bytes 98312 | tf_op jit(solution)/shard_map/ppermute | solution.py:23
  85.1 0.9 collective-permute-done.7
  86.0 3.7 %fusion.40 = f32[128,1,64]{2,1,0:T(1,128)S(1)} fusion(f32[64,128,1]{0,2,1:T(1,128)S(1)} %bitcast.257, f32[64,64,128]{0,1,2:T(8,128)S(1)} %copy-done.2), kind=kOutput, calls=%fused_computation.95 | convolution fusion | flops 6291456 | bytes 2162688 | tf_op jit(solution)/shard_map/abl,bl->al/dot_general | solution.py:27
  89.7 0.1 bitcast_select_fusion
  89.8 0.7 copy.20
  (24 shorter events, 0.2 us)
Async XLA Ops:
  0.9 19.4 %collective-permute-start = (f32[1,64,128]{1,2,0:T(8,128)S(1)}, f32[1,64,128]{1,2,0:T(8,128)S(1)}, u32[]{:S(2)}, u32[]{:S(2)}) collective-permute-start(f32[1,64,128]{1,2,0:T(8,128)S(1)} %copy.11), channel_id=1, source_target_pairs={{0,2},{2,4},{4,6},{6,8},{8,10},{10,12},{12,14},{14,16},{16,18},{18... | collective-permute-start | bytes 98312 | tf_op jit(solution)/shard_map/ppermute | solution.py:14
  3.0 17.3 %collective-permute-start.1 = (f32[1,64,128]{1,2,0:T(8,128)S(1)}, f32[1,64,128]{1,2,0:T(8,128)S(1)}, u32[]{:S(2)}, u32[]{:S(2)}) collective-permute-start(f32[1,64,128]{1,2,0:T(8,128)S(1)} %copy.11), channel_id=1, source_target_pairs={{2,0},{4,2},{6,4},{8,6},{10,8},{12,10},{14,12},{16,14},{18,16},{20... | collective-permute-start | bytes 98312 | tf_op jit(solution)/shard_map/ppermute | solution.py:15
  14.3 5.9 %copy-start.3 = (f32[1,64,128]{2,1,0:T(8,128)S(1)}, f32[1,64,128]{2,1,0:T(8,128)}, u32[]{:S(2)}) copy-start(f32[1,64,128]{2,1,0:T(8,128)} %param.11) | copy-start | bytes 98308
  23.1 12.9 %collective-permute-start.2 = (f32[64,128]{0,1:T(8,128)S(1)}, f32[64,128]{0,1:T(8,128)S(1)}, u32[]{:S(2)}, u32[]{:S(2)}) collective-permute-start(f32[64,128]{0,1:T(8,128)S(1)} %get-tuple-element.8), channel_id=1, source_target_pairs={{0,1},{2,3},{4,5},{6,7},{8,9},{10,11},{12,13},{14,15},{16,17},{18,... | collective-permute-start | bytes 98312 | tf_op jit(solution)/shard_map/ppermute | solution.py:23
  36.0 5.5 %copy-start = (f32[64,64,128]{0,1,2:T(8,128)S(1)}, f32[64,64,128]{0,1,2:T(8,128)}, u32[]{:S(2)}) copy-start(f32[64,64,128]{0,1,2:T(8,128)} %copy.39) | copy-start | bytes 6291460
  36.0 12.3 %copy-start.4 = (s32[128]{0:T(128)S(1)}, s32[128]{0:T(128)}, u32[]{:S(2)}) copy-start(s32[128]{0:T(128)} %param.19) | copy-start | bytes 1540
  45.2 7.7 %collective-permute-start.3 = (f32[64,128]{0,1:T(8,128)S(1)}, f32[64,128]{0,1:T(8,128)S(1)}, u32[]{:S(2)}, u32[]{:S(2)}) collective-permute-start(f32[64,128]{0,1:T(8,128)S(1)} %add_bitcast_fusion.1), channel_id=1, source_target_pairs={{1,0},{3,2},{5,4},{7,6},{9,8},{11,10},{13,12},{15,14},{17,16},{19,... | collective-permute-start | bytes 98312 | tf_op jit(solution)/shard_map/ppermute | solution.py:23
  58.3 9.3 %collective-permute-start.4 = (f32[1,64,128]{1,2,0:T(8,128)S(1)}, f32[1,64,128]{1,2,0:T(8,128)S(1)}, u32[]{:S(2)}, u32[]{:S(2)}) collective-permute-start(f32[1,64,128]{1,2,0:T(8,128)S(1)} %bitcast_select_fusion.5), channel_id=1, source_target_pairs={{0,2},{2,4},{4,6},{6,8},{8,10},{10,12},{12,14},{14,16},{16,18},{18... | collective-permute-start | bytes 98312 | tf_op jit(solution)/shard_map/ppermute | solution.py:14
  58.4 9.2 %collective-permute-start.5 = (f32[1,64,128]{1,2,0:T(8,128)S(1)}, f32[1,64,128]{1,2,0:T(8,128)S(1)}, u32[]{:S(2)}, u32[]{:S(2)}) collective-permute-start(f32[1,64,128]{1,2,0:T(8,128)S(1)} %bitcast_select_fusion.5), channel_id=1, source_target_pairs={{2,0},{4,2},{6,4},{8,6},{10,8},{12,10},{14,12},{16,14},{18,16},{20... | collective-permute-start | bytes 98312 | tf_op jit(solution)/shard_map/ppermute | solution.py:15
  70.2 9.0 %copy-start.1 = (f32[64,64,128]{0,1,2:T(8,128)S(1)}, f32[64,64,128]{0,1,2:T(8,128)}, u32[]{:S(2)}) copy-start(f32[64,64,128]{0,1,2:T(8,128)} %copy.39) | copy-start | bytes 6291460
  70.4 3.4 %collective-permute-start.6 = (f32[64,128]{0,1:T(8,128)S(1)}, f32[64,128]{0,1:T(8,128)S(1)}, u32[]{:S(2)}, u32[]{:S(2)}) collective-permute-start(f32[64,128]{0,1:T(8,128)S(1)} %get-tuple-element.6), channel_id=1, source_target_pairs={{0,1},{2,3},{4,5},{6,7},{8,9},{10,11},{12,13},{14,15},{16,17},{18,... | collective-permute-start | bytes 98312 | tf_op jit(solution)/shard_map/ppermute | solution.py:23
  73.8 12.2 %copy-start.2 = (f32[64,64,128]{0,1,2:T(8,128)S(1)}, f32[64,64,128]{0,1,2:T(8,128)}, u32[]{:S(2)}) copy-start(f32[64,64,128]{0,1,2:T(8,128)} %copy.56) | copy-start | bytes 6291460
  83.0 3.0 %collective-permute-start.7 = (f32[64,128]{0,1:T(8,128)S(1)}, f32[64,128]{0,1:T(8,128)S(1)}, u32[]{:S(2)}, u32[]{:S(2)}) collective-permute-start(f32[64,128]{0,1:T(8,128)S(1)} %add_bitcast_fusion), channel_id=1, source_target_pairs={{1,0},{3,2},{5,4},{7,6},{9,8},{11,10},{13,12},{15,14},{17,16},{19,... | collective-permute-start | bytes 98312 | tf_op jit(solution)/shard_map/ppermute | solution.py:23
where the time goes:
time: 90.8 us; the launch traced here: 90.5 us
  matrix products  27.2 us (30%)
  starting transfers between devices  26.3 us (29%)
  local copies, waits for them, and re-layouts  24.2 us (27%)
  other arithmetic  7.41 us (8%)
  waiting for transfers between devices  5.07 us (6%)
    dot_general x6, matrix products, matvec(): return jnp.einsum('abl,bl->al', mat, vec, precision=lax.Precision.HIGHEST)  27.2 us
    ppermute x2, starting transfers between devices, padded(): after = lax.ppermute(first, axis, down)  16 us
    ppermute x4, starting transfers between devices, from_behind(): lax.ppermute(value, axis, [(source, source + steps) for source in range(f...  8.13 us
    squeeze x1, local copies, waits for them, and re-layouts, line_solve(): pivot_inv[row]  5.61 us
    mul x1, local copies, waits for them, and re-layouts, shards(): forward_maps = [-active[0][None, None, :] * lower[0]]  5.61 us
    unnamed x1, other arithmetic  5.28 us
    gather x8, local copies, waits for them, and re-layouts, source_of(): total = total - coupling[face] * jnp.take(gathered, positions[face], axis=2)  5.15 us
    mul x1, local copies, waits for them, and re-layouts, shards(): -active[seg_count - 1][None, None, :] * upper_back[seg_count - 1]  4.59 us
  transfers between devices with their start and end apart: 8, of which 3 were waited for; matrix products, arithmetic and copies ran while one was open for 27% of the time, Pallas kernels for 0%

commit v1 on v0

v1 whole, which is shorter than its diff:
```python
import functools

import jax
import jax.numpy as jnp
from jax import lax
from jax.experimental import pallas as pl
from jax.experimental.pallas import tpu as pltpu
from jax.sharding import PartitionSpec as P

MESH = pl.DeviceIdType.MESH
BLOCK = 64
FACES = 4
LANES = 128
SUB = 8
TILES = BLOCK // SUB


def tile(j):
    return pl.ds(pl.multiple_of(j * SUB, SUB), SUB)


def fold(parts, masks):
    step = 1
    for mask in masks:
        merged = []
        for base in range(0, len(parts), 2):
            a, b = parts[base], parts[base + 1]
            merged.append(jnp.where(mask, a, b) + pltpu.roll(jnp.where(mask, b, a), step, 0))
        parts = merged
        step *= 2
    return parts[0]


def tree(terms):
    while len(terms) > 1:
        terms = [terms[i] + terms[i + 1] for i in range(0, len(terms) - 1, 2)] + terms[len(terms) & ~1:]
    return terms[0]


def products(pairs, finish, masks):
    vecs = [[vec[pl.ds(SUB * b, SUB), :] for b in range(TILES)] for _, vec in pairs]

    def body(j, _):
        parts = []
        for a in range(SUB):
            row = j * SUB + a
            terms = []
            for (mat, _), vec in zip(pairs, vecs):
                terms.append(tree([mat[row, pl.ds(SUB * b, SUB), :] * vec[b] for b in range(TILES)]))
            parts.append(terms[0] if len(terms) == 1 else terms[0] - terms[1])
        finish(j, fold(parts, masks))
        return 0

    lax.fori_loop(0, TILES, body, 0)


def kernel(groups, rhs, prev, lower, pivot, upper, coupling, neighbours, counts, colour, out,
           lo, p1, p0, up, v0, v1, r0, r1, c0, c1, nb, cnt, col, h1, h2, f0, f1, x0, x1, cur0, cur1, gy, gx, gc,
           loc, wsend, wrecv, s1, q1, s2, q2):
    s = lax.axis_index("surf")
    w = lax.axis_index("wall")
    right = lax.rem(s + 1, groups)
    left = lax.rem(s + groups - 1, groups)
    sub = lax.broadcasted_iota(jnp.int32, (SUB, LANES), 0)
    masks = [(sub & 1) == 0, (sub & 2) == 0, (sub & 4) == 0]
    barrier = pltpu.get_barrier_semaphore()

    def wall_copy(src, dst, i, to):
        return pltpu.make_async_remote_copy(src_ref=src, dst_ref=dst, send_sem=wsend.at[i], recv_sem=wrecv.at[i],
                                            device_id=(s, to), device_id_type=MESH)

    down = [
        wall_copy(prev.at[0], v0, 0, 1),
        wall_copy(rhs.at[0], r0, 1, 1),
        wall_copy(coupling.at[:, 0], c0, 2, 1),
        wall_copy(pivot.at[0], p0, 3, 1),
        wall_copy(upper.at[0], up, 4, 1),
    ]
    back_cur = wall_copy(cur0, gc, 5, 0)
    back_y = wall_copy(f0, gy, 6, 0)
    back_x = wall_copy(x1, gx, 7, 0)

    def local(src, dst, i):
        return pltpu.make_async_copy(src, dst, loc.at[i])

    @pl.when(w == 0)
    def _():
        pl.semaphore_signal(barrier, inc=1, device_id=(s, 1), device_id_type=MESH)
        pl.semaphore_wait(barrier, 1)
        for c in down:
            c.start()
        mine = [local(pivot.at[0], p0, 0), local(upper.at[0], up, 1), local(colour, col, 2), local(counts, cnt, 3)]
        for c in mine:
            c.start()
        for c in mine:
            c.wait()
        back_cur.wait_recv()
        back_y.wait_recv()

        def keep(j, t):
            f1[tile(j), :] = t

        products([(p0, gy)], keep, masks)
        second = jnp.broadcast_to(col[...] == 1, (SUB, LANES))
        alive = jnp.broadcast_to((cnt[...] > 0).astype(jnp.float32), (SUB, LANES))
        back_x.wait_recv()

        def last(j, t):
            out[0, tile(j), :] = jnp.where(second, alive * (f1[tile(j), :] - t), gc[tile(j), :])

        products([(up, gx)], last, masks)
        for c in down:
            c.wait_send()

    @pl.when(w == 1)
    def _():
        pl.semaphore_signal(barrier, inc=1, device_id=(s, 0), device_id_type=MESH)
        pl.semaphore_signal(barrier, inc=1, device_id=(right, 1), device_id_type=MESH)
        pl.semaphore_signal(barrier, inc=1, device_id=(left, 1), device_id_type=MESH)
        mine = [local(prev.at[0], v1, 0), local(rhs.at[0], r1, 1), local(coupling.at[:, 0], c1, 2),
                local(neighbours, nb, 3), local(counts, cnt, 4), local(colour, col, 5),
                local(lower.at[0], lo, 6), local(pivot.at[0], p1, 7)]
        for c in mine:
            c.start()
        pl.semaphore_wait(barrier, 3)

        def surf_copy(src, buf, send, recv, side, row):
            return pltpu.make_async_remote_copy(
                src_ref=src, dst_ref=buf.at[side, row], send_sem=send.at[side, row], recv_sem=recv.at[side, row],
                device_id=(right if side == 0 else left, 1), device_id_type=MESH)

        first = [[surf_copy(v, h1, s1, q1, side, row) for row, v in ((0, v0), (1, v1))] for side in (0, 1)]
        again = [[surf_copy(v, h2, s2, q2, side, row) for row, v in ((0, cur0), (1, cur1))] for side in (0, 1)]
        mine[0].wait()
        first[0][1].start()
        first[1][1].start()
        down[0].wait_recv()
        first[0][0].start()
        first[1][0].start()
        for c in mine[1:6]:
            c.wait()
        down[1].wait_recv()
        down[2].wait_recv()

        here = []
        above = []
        below = []
        lanes = []
        for k in range(FACES):
            line = nb[pl.ds(k, 1), :]
            lanes.append(jnp.broadcast_to(line & (LANES - 1), (SUB, LANES)))
            owner = jnp.broadcast_to(line >> 7, (SUB, LANES))
            here.append(owner == s)
            above.append(owner == right)
            below.append(owner == left)
        alive0 = jnp.broadcast_to((cnt[...] > 0).astype(jnp.float32), (SUB, LANES))
        alive1 = jnp.broadcast_to((cnt[...] > 1).astype(jnp.float32), (SUB, LANES))
        colours = jnp.broadcast_to(col[...], (SUB, LANES))
        rows = ((r0, c0, f0), (r1, c1, f1))

        def pick(value, lane):
            return jnp.take_along_axis(value, lane, axis=1, mode="promise_in_bounds")

        def own_part(fields):
            def body(j, _):
                for (rr, cc, ff), field in zip(rows, fields):
                    total = rr[tile(j), :]
                    value = field[tile(j), :]
                    for k in range(FACES):
                        total = total - cc[k, tile(j), :] * jnp.where(here[k], pick(value, lanes[k]), 0.0)
                    ff[tile(j), :] = total
                return 0

            lax.fori_loop(0, TILES, body, 0)

        def far_part(halo):
            def body(j, _):
                for row, (rr, cc, ff) in enumerate(rows):
                    total = ff[tile(j), :]
                    lval = halo[0, row, tile(j), :]
                    rval = halo[1, row, tile(j), :]
                    for k in range(FACES):
                        far = jnp.where(above[k], pick(rval, lanes[k]),
                                        jnp.where(below[k], pick(lval, lanes[k]), 0.0))
                        total = total - cc[k, tile(j), :] * far
                    ff[tile(j), :] = total * alive0 if row == 0 else total
                return 0

            lax.fori_loop(0, TILES, body, 0)

        def forward(j, t):
            f1[tile(j), :] = alive1 * (f1[tile(j), :] - t)

        def solved1(j, t):
            x1[tile(j), :] = alive1 * t

        own_part((v0, v1))
        mine[6].wait()
        mine[7].wait()
        for row in (1, 0):
            for side in (0, 1):
                first[side][row].wait_recv()
        far_part(h1)
        products([(lo, f0)], forward, masks)

        def first1(j, t):
            cur1[tile(j), :] = jnp.where(colours == 0, alive1 * t, v1[tile(j), :])

        def solved1_full(j, t):
            x1[tile(j), :] = alive1 * t
            first1(j, t)

        products([(p1, f1)], solved1_full, masks)
        again[0][1].start()
        again[1][1].start()
        down[3].wait_recv()
        down[4].wait_recv()

        def first0(j, t):
            cur0[tile(j), :] = jnp.where(colours == 0, alive0 * t, v0[tile(j), :])

        products([(p0, f0), (up, x1)], first0, masks)
        again[0][0].start()
        again[1][0].start()
        back_cur.start()
        own_part((cur0, cur1))
        for row in (1, 0):
            for side in (0, 1):
                again[side][row].wait_recv()
        far_part(h2)
        back_y.start()
        products([(lo, f0)], forward, masks)
        products([(p1, f1)], solved1, masks)
        back_x.start()

        def body(j, _):
            out[0, tile(j), :] = jnp.where(colours == 1, x1[tile(j), :], cur1[tile(j), :])
            return 0

        lax.fori_loop(0, TILES, body, 0)
        for pair in first + again:
            for c in pair:
                c.wait_send()
        back_cur.wait_send()
        back_y.wait_send()
        back_x.wait_send()


def shards(groups, rhs, prev_solution, lower, pivot_inv, upper_back, coupling, neighbours, counts, colour):
    plane = pltpu.VMEM((BLOCK, LANES), jnp.float32)
    matrix = pltpu.VMEM((BLOCK, BLOCK, LANES), jnp.float32)
    faces = pltpu.VMEM((FACES, BLOCK, LANES), jnp.float32)
    halo = pltpu.VMEM((2, 2, BLOCK, LANES), jnp.float32)
    line = pltpu.VMEM((1, LANES), jnp.int32)
    dma = pltpu.SemaphoreType.DMA
    return pl.pallas_call(
        functools.partial(kernel, groups),
        out_shape=jax.ShapeDtypeStruct((1, BLOCK, LANES), jnp.float32),
        in_specs=[pl.BlockSpec(memory_space=pltpu.HBM)] * 9,
        out_specs=pl.BlockSpec(memory_space=pltpu.VMEM),
        scratch_shapes=[matrix] * 4 + [plane] * 4 + [faces] * 2
        + [pltpu.VMEM((FACES, LANES), jnp.int32), line, line] + [halo] * 2 + [plane] * 9
        + [dma((8,)), dma((8,)), dma((8,))] + [dma((2, 2))] * 4,
        compiler_params=pltpu.CompilerParams(collective_id=0, has_side_effects=True, vmem_limit_bytes=56 << 20),
    )(rhs, prev_solution, lower, pivot_inv, upper_back, coupling, neighbours,
      counts.reshape(1, LANES), colour.reshape(1, LANES))


def solution(mesh):
    placed = (
        P("wall", None, "surf"),
        P("wall", None, "surf"),
        P("wall", None, None, "surf"),
        P("wall", None, None, "surf"),
        P("wall", None, None, "surf"),
        P(None, "wall", None, "surf"),
        P(None, "surf"),
        P("surf"),
        P("surf"),
    )
    return jax.shard_map(
        functools.partial(shards, mesh.shape["surf"]), mesh=mesh, in_specs=placed, out_specs=P("wall", None, "surf"),
        check_vma=False,
    )
```

time: 90.8 us -> 27.2 us (0.30)
  matrix products: 27.2 us -> 0 us
  starting transfers between devices: 26.3 us -> 0 us
  Pallas kernels: 0 us -> 25.7 us
  local copies, waits for them, and re-layouts: 24.2 us -> 1.38 us
  other arithmetic: 7.41 us -> 0 us
  waiting for transfers between devices: 5.07 us -> 0 us
    dot_general x6 -> x0, matrix products: 27.2 us -> none  [matvec(): return jnp.einsum('abl,bl->al', mat, vec, precision=lax.Precision.HIGHEST)]
    ppermute x8 -> x0, starting transfers between devices: 26.3 us -> none  [the longest x2 16 us: padded(): after = lax.ppermute(first, axis, down)]
    pallas_call x0 -> x1, Pallas kernels: none -> 25.7 us  [shards(): pl.pallas_call(functools.partial(kernel, groups), out_shape=jax.ShapeDtyp...]
    mul x2 -> x0, local copies, waits for them, and re-layouts: 10.2 us -> none  [the longest x1 5.61 us: shards(): forward_maps = [-active[0][None, None, :] * lower[0]]]
    squeeze x1 -> x0, local copies, waits for them, and re-layouts: 5.61 us -> none  [line_solve(): pivot_inv[row]]
    unnamed x1 -> x0, other arithmetic: 5.28 us -> none
    gather x8 -> x0, local copies, waits for them, and re-layouts: 5.15 us -> none  [source_of(): total = total - coupling[face] * jnp.take(gathered, positions[face], axis=2)]
    ppermute x8 -> x0, waiting for transfers between devices: 5.07 us -> none  [the longest x4 2.73 us: from_behind(): lax.ppermute(value, axis, [(source, source + steps) for source in range(f...]
  transfers between devices with their start and end apart: 8 -> 0, of which waited for: 3 -> 0; matrix products, arithmetic and copies ran while one was open for 27% -> 0% of each run, Pallas kernels for 0% -> 0%
where the time goes in v1:
time: 27.2 us; the launch traced here: 27.1 us
  Pallas kernels  25.7 us (94%)
  local copies, waits for them, and re-layouts  1.38 us (5%)
    pallas_call x1, Pallas kernels, shards(): pl.pallas_call(functools.partial(kernel, groups), out_shape=jax.ShapeDtyp...  25.7 us
    unnamed x1, local copies, waits for them, and re-layouts  1.38 us

profile of v1, /device:TPU:1, one launch (start us, length us, event | category | flops | bytes accessed | tf_op | source)
XLA Modules:
  0.0 27.1 jit_solution(2231732974926688162)
XLA Ops:
  0.0 25.7 %shard_map.91 = f32[1,64,128]{2,1,0:T(8,128)} custom-call(f32[1,64,128]{2,1,0:T(8,128)} %rhs.1, f32[1,64,128]{2,1,0:T(8,128)} %prev.1, f32[1,64,64,128]{3,2,1,0:T(8,128)} %lower.1, f32[1,64,64,128]{3,2,1,0:T(8,128)} %pivot.1, f32[1,64,64,128]{3,2,1,0:T(8,128)} %upper.1, f32[4,1,64,128]{3,2,1,0:T(8,128)} %coupling.1, s32[4,128]{1,0:T(4,128)} %neighbours.1, ...), custom_call_target="tpu_custom_call" | custom-call | tf_op jit(solution)/shard_map/pallas_call | solution.py:256
  25.7 1.4 %copy.11 = f32[1,64,128]{2,1,0:T(8,128)} copy(f32[1,64,128]{2,1,0:T(8,128)} %shard_map.91) | data formatting | bytes 65536

commit v2 on v1

v2 whole, which is shorter than its diff:
```python
import functools

import jax
import jax.numpy as jnp
from jax import lax
from jax.experimental import pallas as pl
from jax.experimental.pallas import tpu as pltpu
from jax.sharding import PartitionSpec as P

MESH = pl.DeviceIdType.MESH
BLOCK = 64
FACES = 4
LANES = 128
SUB = 8
TILES = BLOCK // SUB
ROW = 4
PLANE = 16


def tile(j):
    return pl.ds(pl.multiple_of(j * SUB, SUB), SUB)


def fold(parts, masks):
    step = 1
    for mask in masks:
        merged = []
        for base in range(0, len(parts), 2):
            a, b = parts[base], parts[base + 1]
            merged.append(jnp.where(mask, a, b) + pltpu.roll(jnp.where(mask, b, a), step, 0))
        parts = merged
        step *= 2
    return parts[0]


def tree(terms):
    while len(terms) > 1:
        terms = [terms[i] + terms[i + 1] for i in range(0, len(terms) - 1, 2)] + terms[len(terms) & ~1:]
    return terms[0]


def products(pairs, finish, masks):
    vecs = [[vec[pl.ds(SUB * b, SUB), :] for b in range(TILES)] for _, vec in pairs]

    def body(j, _):
        parts = []
        for a in range(SUB):
            row = j * SUB + a
            terms = []
            for (mat, _), vec in zip(pairs, vecs):
                terms.append(tree([mat[row, pl.ds(SUB * b, SUB), :] * vec[b] for b in range(TILES)]))
            parts.append(terms[0] if len(terms) == 1 else terms[0] - terms[1])
        finish(j, fold(parts, masks))
        return 0

    lax.fori_loop(0, TILES, body, 0, unroll=TILES)


def kernel(groups, rhs, prev, lower, pivot, upper, coupling, neighbours, counts, colour, out,
           mat_a, mat_b, v0, v1, r0, r1, c0, c1, nb, cnt, col, h1, h2, f0, f1, x1, cur0, cur1, gy, gx, held, hop,
           loc, wsend, wrecv, s1, q1, s2, q2, rsend, rrecv, ready):
    s = lax.axis_index("surf")
    w = lax.axis_index("wall")
    right = lax.rem(s + 1, groups)
    left = lax.rem(s + groups - 1, groups)
    place = lax.rem(s, ROW)
    last_line = groups - 1
    sub = lax.broadcasted_iota(jnp.int32, (SUB, LANES), 0)
    masks = [(sub & 1) == 0, (sub & 2) == 0, (sub & 4) == 0]
    barrier = pltpu.get_barrier_semaphore()

    def signal(sem, to, core):
        pl.semaphore_signal(sem, inc=1, device_id=(to, core), device_id_type=MESH)

    def local(src, dst, i):
        return pltpu.make_async_copy(src, dst, loc.at[i])

    def wall_copy(src, dst, i, to):
        return pltpu.make_async_remote_copy(src_ref=src, dst_ref=dst, send_sem=wsend.at[i], recv_sem=wrecv.at[i],
                                            device_id=(s, to), device_id_type=MESH)

    def surf_copy(src, buf, send, recv, side, row):
        return pltpu.make_async_remote_copy(
            src_ref=src, dst_ref=buf.at[side, row], send_sem=send.at[side], recv_sem=recv.at[side, row],
            device_id=(right if side == 0 else left, 1), device_id_type=MESH)

    down = [wall_copy(prev.at[0], v0, 0, 1), wall_copy(rhs.at[0], r0, 1, 1), wall_copy(coupling.at[:, 0], c0, 2, 1)]
    down_cur = wall_copy(cur0, held, 3, 1)
    back_y = [wall_copy(f0.at[i], gy.at[i], 4 + i, 0) for i in (0, 1)]
    back_x = [wall_copy(x1.at[i], gx.at[i], 6 + i, 0) for i in (0, 1)]

    def send_prev(row, copies):
        copies[0].start()

        @pl.when((s != 0) & ((s != last_line) | (row == 0)))
        def _():
            copies[1].start()

    step1, step2 = ROW - 1, PLANE - 1

    def relay(src, dst, row, to, recv):
        return pltpu.make_async_remote_copy(
            src_ref=src, dst_ref=dst, send_sem=rsend.at[row], recv_sem=recv, device_id=(to, 1), device_id_type=MESH)

    start = [relay(prev.at[0], hop.at[row], row, step1, rrecv.at[row]) for row in (0, 1)]
    middle = [relay(hop.at[row], hop.at[row], row, step2, rrecv.at[row]) for row in (0, 1)]
    end = [relay(hop.at[row], h1.at[1, row], row, last_line, q1.at[1, row]) for row in (0, 1)]

    def finish_sends(first, again):
        for c in [first[0]] + again:
            c.wait_send()

        @pl.when(s != 0)
        def _():
            first[1].wait_send()

    @pl.when(w == 0)
    def _():
        mine = [local(prev.at[0], v0, 0), local(colour, col, 1), local(counts, cnt, 2),
                local(pivot.at[0], mat_a, 3), local(upper.at[0], mat_b, 4)]
        pl.semaphore_wait(barrier, 3)

        @pl.when(s == 0)
        def _():
            start[0].start()

        first = [surf_copy(prev.at[0], h1, s1, q1, side, 0) for side in (0, 1)]
        again = [surf_copy(cur0, h2, s2, q2, side, 0) for side in (0, 1)]
        send_prev(0, first)
        for c in down:
            c.start()
        for c in mine:
            c.start()
        for c in mine:
            c.wait()
        alive = jnp.broadcast_to((cnt[...] > 0).astype(jnp.float32), (SUB, LANES))
        colours = jnp.broadcast_to(col[...], (SUB, LANES))

        def keep(j, t):
            held[tile(j), :] = t

        def first0(j, t):
            cur0[tile(j), :] = jnp.where(colours == 0, alive * (held[tile(j), :] - t), v0[tile(j), :])

        def second0(j, t):
            out[0, tile(j), :] = jnp.where(colours == 1, alive * (held[tile(j), :] - t), cur0[tile(j), :])

        back_y[0].wait_recv()
        products([(mat_a, gy.at[0])], keep, masks)
        back_x[0].wait_recv()
        products([(mat_b, gx.at[0])], first0, masks)
        for c in again:
            c.start()
        down_cur.start()
        back_y[1].wait_recv()
        products([(mat_a, gy.at[1])], keep, masks)
        back_x[1].wait_recv()
        products([(mat_b, gx.at[1])], second0, masks)
        finish_sends(first, again + down + [down_cur])

        @pl.when(s == 0)
        def _():
            start[0].wait_send()


    @pl.when(w == 1)
    def _():
        def greet(to, core):
            signal(barrier, to, core)

        greet(s, 0)
        greet(left, 0)
        greet(left, 1)

        @pl.when(s != last_line)
        def _():
            greet(right, 0)

        @pl.when(s < last_line - 1)
        def _():
            greet(right, 1)

        @pl.when(s == step1)
        def _():
            greet(0, 0)
            greet(0, 1)
            greet(step2, 1)

        @pl.when(s == step2)
        def _():
            greet(last_line, 1)

        mine = [local(prev.at[0], v1, 0), local(rhs.at[0], r1, 1), local(coupling.at[:, 0], c1, 2),
                local(neighbours, nb, 3), local(counts, cnt, 4), local(colour, col, 5),
                local(lower.at[0], mat_a, 6), local(pivot.at[0], mat_b, 7)]
        ends = (s == 0) | (s == last_line)
        pl.semaphore_wait(barrier, jnp.where(ends, 1, 2) + jnp.where(ends | (s == step2), 1, 0))

        @pl.when(s == last_line)
        def _():
            signal(ready.at[0], step2, 1)

        @pl.when(s == step2)
        def _():
            signal(ready.at[0], step1, 1)

        @pl.when(s == last_line - 1)
        def _():
            signal(ready.at[1], last_line, 1)

        @pl.when(s == 0)
        def _():
            start[1].start()

        first = [surf_copy(prev.at[0], h1, s1, q1, side, 1) for side in (0, 1)]
        again = [surf_copy(cur1, h2, s2, q2, side, 1) for side in (0, 1)]
        send_prev(1, first)
        for c in mine:
            c.start()

        @pl.when(s == last_line)
        def _():
            pl.semaphore_wait(ready.at[1], 1)
            first[1].start()

        def pass_on(arriving, leaving):
            pl.semaphore_wait(ready.at[0], 1)
            for row in (0, 1):
                arriving[row].wait_recv()
                leaving[row].start()

        @pl.when(s == step1)
        def _():
            pass_on(start, middle)

        @pl.when(s == step2)
        def _():
            pass_on(middle, end)

        mine[0].wait()
        down[0].wait_recv()
        for c in mine[1:6]:
            c.wait()
        down[1].wait_recv()
        down[2].wait_recv()

        slow = jnp.where(place == ROW - 1, 1, 0)
        quick = 1 - slow
        slow_line = jnp.where(slow == 1, right, left)
        quick_line = jnp.where(slow == 1, left, right)
        owners = ([], [], [])
        lanes = []
        for k in range(FACES):
            line = nb[pl.ds(k, 1), :]
            lanes.append(jnp.broadcast_to(line & (LANES - 1), (SUB, LANES)))
            owner = jnp.broadcast_to(line >> 7, (SUB, LANES))
            for masks_of, holder in zip(owners, (s, quick_line, slow_line)):
                masks_of.append(owner == holder)
        here, near, far = owners
        alive0 = jnp.broadcast_to((cnt[...] > 0).astype(jnp.float32), (SUB, LANES))
        alive1 = jnp.broadcast_to((cnt[...] > 1).astype(jnp.float32), (SUB, LANES))
        colours = jnp.broadcast_to(col[...], (SUB, LANES))
        coef = (c0, c1)

        def minus(start, row, j, value, held_by):
            for k in range(FACES):
                taken = jnp.take_along_axis(value, lanes[k], axis=1, mode="promise_in_bounds")
                start = start - coef[row][k, tile(j), :] * jnp.where(held_by[k], taken, 0.0)
            return start

        def own_part(total, given, row, field):
            def body(j, _):
                total[tile(j), :] = minus(given[tile(j), :], row, j, field[tile(j), :], here)
                return 0

            lax.fori_loop(0, TILES, body, 0, unroll=TILES)

        def side_part(total, halo, side, held_by, row, scale):
            def body(j, _):
                value = minus(total[tile(j), :], row, j, halo[side, row, tile(j), :], held_by)
                total[tile(j), :] = value if scale is None else scale * value
                return 0

            lax.fori_loop(0, TILES, body, 0, unroll=TILES)

        def wait(buf, recv, side, row):
            pltpu.make_async_copy(buf.at[side, row], buf.at[side, row], recv.at[side, row]).wait()

        def solve(phase, halo, recv, finish):
            y0 = f0.at[phase]
            for row, total in ((1, f1), (0, y0)):
                wait(halo, recv, quick, row)
                side_part(total, halo, quick, near, row, None)
            wait(halo, recv, slow, 1)
            wait(halo, recv, slow, 0)
            side_part(y0, halo, slow, far, 0, alive0)
            back_y[phase].start()

            def forward(j, t):
                source = minus(f1[tile(j), :], 1, j, halo[slow, 1, tile(j), :], far)
                f1[tile(j), :] = alive1 * (source - t)

            products([(mat_a, y0)], forward, masks)
            products([(mat_b, f1)], finish, masks)
            back_x[phase].start()

        def first1(j, t):
            x1[0, tile(j), :] = alive1 * t
            cur1[tile(j), :] = jnp.where(colours == 0, alive1 * t, v1[tile(j), :])

        def second1(j, t):
            x1[1, tile(j), :] = alive1 * t
            out[0, tile(j), :] = jnp.where(colours == 1, alive1 * t, cur1[tile(j), :])

        own_part(f0.at[0], r0, 0, v0)
        own_part(f1, r1, 1, v1)
        mine[6].wait()
        mine[7].wait()
        solve(0, h1, q1, first1)
        for c in again:
            c.start()
        own_part(f1, r1, 1, cur1)
        down_cur.wait_recv()
        own_part(f0.at[1], r0, 0, held)
        solve(1, h2, q2, second1)
        finish_sends(first, again + back_y + back_x)

        @pl.when(s == 0)
        def _():
            start[1].wait_send()

        @pl.when(s == step1)
        def _():
            for c in middle:
                c.wait_send()

        @pl.when(s == step2)
        def _():
            for c in end:
                c.wait_send()


def shards(groups, rhs, prev_solution, lower, pivot_inv, upper_back, coupling, neighbours, counts, colour):
    plane = pltpu.VMEM((BLOCK, LANES), jnp.float32)
    matrix = pltpu.VMEM((BLOCK, BLOCK, LANES), jnp.float32)
    faces = pltpu.VMEM((FACES, BLOCK, LANES), jnp.float32)
    halo = pltpu.VMEM((2, 2, BLOCK, LANES), jnp.float32)
    pair = pltpu.VMEM((2, BLOCK, LANES), jnp.float32)
    line = pltpu.VMEM((1, LANES), jnp.int32)
    dma = pltpu.SemaphoreType.DMA
    here = (rhs, prev_solution, lower, pivot_inv, upper_back, coupling, neighbours,
            counts.reshape(1, LANES), colour.reshape(1, LANES))
    return pl.pallas_call(
        functools.partial(kernel, groups),
        out_shape=pltpu.VMEM((1, BLOCK, LANES), jnp.float32),
        in_specs=[pl.BlockSpec(memory_space=pltpu.HBM)] * 9,
        out_specs=pl.BlockSpec(memory_space=pltpu.VMEM),
        scratch_shapes=[matrix] * 2 + [plane] * 4 + [faces] * 2
        + [pltpu.VMEM((FACES, LANES), jnp.int32), line, line] + [halo] * 2
        + [pair, plane, pair, plane, plane, pair, pair, plane, pair]
        + [dma((8,)), dma((8,)), dma((8,))] + [dma((2,)), dma((2, 2))] * 2
        + [dma((2,)), dma((2,)), pltpu.SemaphoreType.REGULAR((2,))],
        compiler_params=pltpu.CompilerParams(collective_id=0, has_side_effects=True, vmem_limit_bytes=16 << 20),
    )(*[pltpu.with_memory_space_constraint(a, pltpu.HBM) for a in here])


def solution(mesh):
    placed = (
        P("wall", None, "surf"),
        P("wall", None, "surf"),
        P("wall", None, None, "surf"),
        P("wall", None, None, "surf"),
        P("wall", None, None, "surf"),
        P(None, "wall", None, "surf"),
        P(None, "surf"),
        P("surf"),
        P("surf"),
    )
    return jax.shard_map(
        functools.partial(shards, mesh.shape["surf"]), mesh=mesh, in_specs=placed, out_specs=P("wall", None, "surf"),
        check_vma=False,
    )
```

time: 27.2 us -> 22 us (0.81)
  Pallas kernels: 25.7 us -> 21.3 us
  local copies, waits for them, and re-layouts: 1.38 us -> 0.62 us
    pallas_call x1, Pallas kernels: 25.7 us -> 21.3 us  [shards(): pl.pallas_call(functools.partial(kernel, groups), out_shape=pltpu.VMEM((1...]
    unnamed x1, local copies, waits for them, and re-layouts: 1.38 us -> 0.62 us
where the time goes in v2:
time: 22 us
  Pallas kernels  21.3 us (97%)
  local copies, waits for them, and re-layouts  0.62 us (3%)
    pallas_call x1, Pallas kernels, shards(): pl.pallas_call(functools.partial(kernel, groups), out_shape=pltpu.VMEM((1...  21.3 us
    unnamed x1, local copies, waits for them, and re-layouts  0.62 us

profile of v2, /device:TPU:1, one launch (start us, length us, event | category | flops | bytes accessed | tf_op | source)
XLA Modules:
  0.0 22.0 jit_solution(12523023049297866800)
XLA Ops:
  0.0 21.3 %shard_map.91 = f32[1,64,128]{2,1,0:T(8,128)S(1)} custom-call(f32[1,64,128]{2,1,0:T(8,128)} %rhs.1, f32[1,64,128]{2,1,0:T(8,128)} %prev.1, f32[1,64,64,128]{3,2,1,0:T(8,128)} %lower.1, f32[1,64,64,128]{3,2,1,0:T(8,128)} %pivot.1, f32[1,64,64,128]{3,2,1,0:T(8,128)} %upper.1, f32[4,1,64,128]{3,2,1,0:T(8,128)} %coupling.1, s32[4,128]{1,0:T(4,128)} %neighbours.1, ...), custom_call_target="tpu_custom_call" | custom-call | tf_op jit(solution)/shard_map/pallas_call | solution.py:353
  21.3 0.6 %copy.11 = f32[1,64,128]{2,1,0:T(8,128)} copy(f32[1,64,128]{2,1,0:T(8,128)S(1)} %shard_map.91) | data formatting | bytes 65536

commit v3 on v2

v3 whole, which is shorter than its diff:
```python
import functools

import jax
import jax.numpy as jnp
from jax import lax
from jax.experimental import pallas as pl
from jax.experimental.pallas import tpu as pltpu
from jax.sharding import PartitionSpec as P

MESH = pl.DeviceIdType.MESH
BLOCK = 64
FACES = 4
LANES = 128
SUB = 8
TILES = BLOCK // SUB
ROW = 4
PLANE = 16


def tile(j):
    return pl.ds(pl.multiple_of(j * SUB, SUB), SUB)


def fold(parts, masks):
    step = 1
    for mask in masks:
        merged = []
        for base in range(0, len(parts), 2):
            a, b = parts[base], parts[base + 1]
            merged.append(jnp.where(mask, a, b) + pltpu.roll(jnp.where(mask, b, a), step, 0))
        parts = merged
        step *= 2
    return parts[0]


def tree(terms):
    while len(terms) > 1:
        terms = [terms[i] + terms[i + 1] for i in range(0, len(terms) - 1, 2)] + terms[len(terms) & ~1:]
    return terms[0]


def products(pairs, finish, masks):
    vecs = [[vec[pl.ds(SUB * b, SUB), :] for b in range(TILES)] for _, vec in pairs]

    def body(j, _):
        parts = []
        for a in range(SUB):
            row = j * SUB + a
            terms = []
            for (mat, _), vec in zip(pairs, vecs):
                terms.append(tree([mat[row, pl.ds(SUB * b, SUB), :] * vec[b] for b in range(TILES)]))
            parts.append(terms[0] if len(terms) == 1 else terms[0] - terms[1])
        finish(j, fold(parts, masks))
        return 0

    lax.fori_loop(0, TILES, body, 0, unroll=TILES)


def kernel(groups, rhs, prev, lower, pivot, upper, coupling, neighbours, counts, colour, out,
           mat_l, mat_p1, mat_p0, mat_u, v0, v1, r0, r1, c0, c1, nb, cnt, col, h1, h2, f0, f1, x1, cur0, cur1, part_t, part_u,
           got_y, got_x, hop, loc, wsend, wrecv, s1, q1, s2, q2, rsend, rrecv, ready):
    s = lax.axis_index("surf")
    w = lax.axis_index("wall")
    right = lax.rem(s + 1, groups)
    left = lax.rem(s + groups - 1, groups)
    place = lax.rem(s, ROW)
    last_line = groups - 1
    sub = lax.broadcasted_iota(jnp.int32, (SUB, LANES), 0)
    masks = [(sub & 1) == 0, (sub & 2) == 0, (sub & 4) == 0]
    barrier = pltpu.get_barrier_semaphore()
    slow = jnp.where(place == ROW - 1, 1, 0)
    quick = 1 - slow
    slow_line = jnp.where(slow == 1, right, left)
    quick_line = jnp.where(slow == 1, left, right)

    def signal(sem, to, core):
        pl.semaphore_signal(sem, inc=1, device_id=(to, core), device_id_type=MESH)

    def local(src, dst, i):
        return pltpu.make_async_copy(src, dst, loc.at[i])

    def wall_copy(src, dst, i, to):
        return pltpu.make_async_remote_copy(src_ref=src, dst_ref=dst, send_sem=wsend.at[i], recv_sem=wrecv.at[i],
                                            device_id=(s, to), device_id_type=MESH)

    def first_copy(side, row):
        return pltpu.make_async_remote_copy(
            src_ref=prev.at[0], dst_ref=h1.at[side, row], send_sem=s1.at[side], recv_sem=q1.at[side, row],
            device_id=(right if side == 0 else left, 1), device_id_type=MESH)

    def again_copy(src, kind, side, core):
        return pltpu.make_async_remote_copy(
            src_ref=src, dst_ref=h2.at[side, kind], send_sem=s2.at[kind, side, core], recv_sem=q2.at[side, kind],
            device_id=(right if side == 0 else left, core), device_id_type=MESH)

    def again_copies(src, kind, core):
        return [again_copy(src, kind, side, core) for side in (0, 1)]

    down = [wall_copy(prev.at[0], v0, 0, 1), wall_copy(rhs.at[0], r0, 1, 1), wall_copy(coupling.at[:, 0], c0, 2, 1),
            wall_copy(upper.at[0], mat_u, 3, 1)]
    down_t = wall_copy(part_t, part_t, 4, 1)
    up = [wall_copy(rhs.at[0], r1, 5, 0), wall_copy(coupling.at[:, 0], c1, 6, 0), wall_copy(lower.at[0], mat_l, 7, 0),
          wall_copy(pivot.at[0], mat_p1, 8, 0)]
    up_cur = wall_copy(cur1, cur1, 9, 0)
    up_y = wall_copy(f0.at[0], got_y, 10, 0)
    up_x = wall_copy(x1, got_x, 11, 0)

    def start_slow_first(copies):
        @pl.when(place == 0)
        def _():
            copies[1].start()
            copies[0].start()

        @pl.when(place != 0)
        def _():
            copies[0].start()
            copies[1].start()

    def send_prev(row, copies):
        copies[0].start()

        @pl.when((s != 0) & ((s != last_line) | (row == 0)))
        def _():
            copies[1].start()

    step1, step2 = ROW - 1, PLANE - 1

    def relay(src, dst, row, to, recv):
        return pltpu.make_async_remote_copy(
            src_ref=src, dst_ref=dst, send_sem=rsend.at[row], recv_sem=recv, device_id=(to, 1), device_id_type=MESH)

    start = [relay(prev.at[0], hop.at[row], row, step1, rrecv.at[row]) for row in (0, 1)]
    middle = [relay(hop.at[row], hop.at[row], row, step2, rrecv.at[row]) for row in (0, 1)]
    end = [relay(hop.at[row], h1.at[1, row], row, last_line, q1.at[1, row]) for row in (0, 1)]

    def finish_sends(first, others):
        for c in [first[0]] + others:
            c.wait_send()

        @pl.when(s != 0)
        def _():
            first[1].wait_send()

    def arrived(buf, recv, side, kind):
        pltpu.make_async_copy(buf.at[side, kind], buf.at[side, kind], recv.at[side, kind]).wait()

    def make_solver():
        owners = ([], [], [])
        lanes = []
        for k in range(FACES):
            line = nb[pl.ds(k, 1), :]
            lanes.append(jnp.broadcast_to(line & (LANES - 1), (SUB, LANES)))
            owner = jnp.broadcast_to(line >> 7, (SUB, LANES))
            for masks_of, holder in zip(owners, (s, quick_line, slow_line)):
                masks_of.append(owner == holder)
        here, near, far = owners
        alive = [jnp.broadcast_to((cnt[...] > row).astype(jnp.float32), (SUB, LANES)) for row in (0, 1)]
        colours = jnp.broadcast_to(col[...], (SUB, LANES))
        coef = (c0, c1)

        def minus(begin, row, j, value, held_by, sign):
            for k in range(FACES):
                taken = jnp.take_along_axis(value, lanes[k], axis=1, mode="promise_in_bounds")
                term = coef[row][k, tile(j), :] * jnp.where(held_by[k], taken, 0.0)
                begin = begin + term if sign > 0 else begin - term
            return begin

        def own_part(total, given, row, field):
            def body(j, _):
                total[tile(j), :] = minus(given[tile(j), :], row, j, field[tile(j), :], here, -1)
                return 0

            lax.fori_loop(0, TILES, body, 0, unroll=TILES)

        def take(total, buf, recv, side, kind, held_by, row, sign, scale=None):
            arrived(buf, recv, side, kind)

            def body(j, _):
                value = minus(total[tile(j), :], row, j, buf[side, kind, tile(j), :], held_by, sign)
                total[tile(j), :] = value if scale is None else scale * value
                return 0

            lax.fori_loop(0, TILES, body, 0, unroll=TILES)

        def solve_first(after_y, finish):
            y0 = f0.at[0]
            take(f1, h1, q1, quick, 1, near, 1, -1)
            take(y0, h1, q1, quick, 0, near, 0, -1)
            take(y0, h1, q1, slow, 0, far, 0, -1, alive[0])
            after_y()
            arrived(h1, q1, slow, 1)

            def forward(j, t):
                source = minus(f1[tile(j), :], 1, j, h1[slow, 1, tile(j), :], far, -1)
                f1[tile(j), :] = alive[1] * (source - t)

            products([(mat_l, y0)], forward, masks)
            products([(mat_p1, f1)], finish, masks)

        def solve_second(finish):
            y0 = f0.at[1]
            for side, held_by in ((quick, near), (slow, far)):
                take(f1, h2, q2, side, 2, held_by, 1, -1)
                take(y0, h2, q2, side, 1, held_by, 0, 1)
                take(y0, h2, q2, side, 0, held_by, 0, -1, alive[0] if held_by is far else None)

            def forward(j, t):
                f1[tile(j), :] = alive[1] * (f1[tile(j), :] - t)

            products([(mat_l, y0)], forward, masks)
            products([(mat_p1, f1)], finish, masks)

        return own_part, solve_first, solve_second, alive, colours

    @pl.when(w == 0)
    def _():
        mine = [local(prev.at[0], v0, 0), local(rhs.at[0], r0, 1), local(coupling.at[:, 0], c0, 2),
                local(neighbours, nb, 3), local(counts, cnt, 4), local(colour, col, 5),
                local(pivot.at[0], mat_p0, 6), local(upper.at[0], mat_u, 7)]
        pl.semaphore_wait(barrier, 3)

        @pl.when(s == 0)
        def _():
            start[0].start()

        first = [first_copy(side, 0) for side in (0, 1)]
        send_prev(0, first)
        for c in down:
            c.start()
        for c in mine:
            c.start()
        for c in mine:
            c.wait()
        own_part, solve_first, solve_second, alive, colours = make_solver()

        def term(j, t):
            part_t[tile(j), :] = jnp.where(colours == 0, alive[0] * t, v0[tile(j), :])

        def first0(j, t):
            cur0[tile(j), :] = part_t[tile(j), :] - jnp.where(colours == 0, alive[0] * t, 0.0)

        def second1(j, t):
            x1[tile(j), :] = alive[1] * t

        def second0(j, t):
            out[0, tile(j), :] = jnp.where(colours == 1, alive[0] * t, cur0[tile(j), :])

        up_y.wait_recv()
        products([(mat_p0, got_y)], term, masks)
        again = [again_copies(part_t, 0, core) for core in (1, 0)]
        start_slow_first(again[0])
        down_t.start()
        start_slow_first(again[1])
        up_x.wait_recv()
        products([(mat_u, got_x)], first0, masks)
        up[0].wait_recv()
        up[1].wait_recv()
        own_part(f0.at[1], r0, 0, cur0)
        up_cur.wait_recv()
        own_part(f1, r1, 1, cur1)
        up[2].wait_recv()
        up[3].wait_recv()
        solve_second(second1)
        products([(mat_p0, f0.at[1]), (mat_u, x1)], second0, masks)
        finish_sends(first, again[0] + again[1] + down + [down_t])

        @pl.when(s == 0)
        def _():
            start[0].wait_send()


    @pl.when(w == 1)
    def _():
        def greet(to, core):
            signal(barrier, to, core)

        greet(s, 0)
        greet(left, 0)
        greet(left, 1)

        @pl.when(s != last_line)
        def _():
            greet(right, 0)

        @pl.when(s < last_line - 1)
        def _():
            greet(right, 1)

        @pl.when(s == step1)
        def _():
            greet(0, 0)
            greet(0, 1)
            greet(step2, 1)

        @pl.when(s == step2)
        def _():
            greet(last_line, 1)

        mine = [local(prev.at[0], v1, 0), local(rhs.at[0], r1, 1), local(coupling.at[:, 0], c1, 2),
                local(neighbours, nb, 3), local(counts, cnt, 4), local(colour, col, 5),
                local(lower.at[0], mat_l, 6), local(pivot.at[0], mat_p1, 7)]
        ends = (s == 0) | (s == last_line)
        pl.semaphore_wait(barrier, jnp.where(ends, 1, 2) + jnp.where(ends | (s == step2), 1, 0))

        @pl.when(s == last_line)
        def _():
            signal(ready.at[0], step2, 1)

        @pl.when(s == step2)
        def _():
            signal(ready.at[0], step1, 1)

        @pl.when(s == last_line - 1)
        def _():
            signal(ready.at[1], last_line, 1)

        @pl.when(s == 0)
        def _():
            start[1].start()

        first = [first_copy(side, 1) for side in (0, 1)]
        send_prev(1, first)
        for c in mine:
            c.start()

        @pl.when(s == last_line)
        def _():
            pl.semaphore_wait(ready.at[1], 1)
            first[1].start()

        def pass_on(arriving, leaving):
            pl.semaphore_wait(ready.at[0], 1)
            for row in (0, 1):
                arriving[row].wait_recv()
                leaving[row].start()

        @pl.when(s == step1)
        def _():
            pass_on(start, middle)

        @pl.when(s == step2)
        def _():
            pass_on(middle, end)

        for c in mine[:6]:
            c.wait()
        own_part, solve_first, solve_second, alive, colours = make_solver()
        own_part(f1, r1, 1, v1)
        for c in down[:3]:
            c.wait_recv()
        for c in up[:3]:
            c.start()
        own_part(f0.at[0], r0, 0, v0)
        mine[6].wait()
        mine[7].wait()

        def first1(j, t):
            x1[tile(j), :] = alive[1] * t
            cur1[tile(j), :] = jnp.where(colours == 0, alive[1] * t, v1[tile(j), :])

        def term(j, t):
            part_u[tile(j), :] = jnp.where(colours == 0, alive[0] * t, 0.0)

        def second1(j, t):
            out[0, tile(j), :] = jnp.where(colours == 1, alive[1] * t, cur1[tile(j), :])

        solve_first(up_y.start, first1)
        again1 = [again_copies(cur1, 2, core) for core in (1, 0)]
        start_slow_first(again1[0])
        down[3].wait_recv()
        products([(mat_u, x1)], term, masks)
        again0 = [again_copies(part_u, 1, core) for core in (1, 0)]
        start_slow_first(again0[0])
        up_x.start()
        up_cur.start()
        start_slow_first(again0[1])
        start_slow_first(again1[1])
        up[3].start()
        own_part(f1, r1, 1, cur1)
        down_t.wait_recv()

        def join(j, _):
            cur0[tile(j), :] = part_t[tile(j), :] - part_u[tile(j), :]
            return 0

        lax.fori_loop(0, TILES, join, 0, unroll=TILES)
        own_part(f0.at[1], r0, 0, cur0)
        solve_second(second1)
        finish_sends(first, up + [up_cur, up_y, up_x] + again0[0] + again0[1] + again1[0] + again1[1])

        @pl.when(s == 0)
        def _():
            start[1].wait_send()

        @pl.when(s == step1)
        def _():
            for c in middle:
                c.wait_send()

        @pl.when(s == step2)
        def _():
            for c in end:
                c.wait_send()


def shards(groups, rhs, prev_solution, lower, pivot_inv, upper_back, coupling, neighbours, counts, colour):
    plane = pltpu.VMEM((BLOCK, LANES), jnp.float32)
    matrix = pltpu.VMEM((BLOCK, BLOCK, LANES), jnp.float32)
    faces = pltpu.VMEM((FACES, BLOCK, LANES), jnp.float32)
    pair = pltpu.VMEM((2, BLOCK, LANES), jnp.float32)
    line = pltpu.VMEM((1, LANES), jnp.int32)
    dma = pltpu.SemaphoreType.DMA
    here = (rhs, prev_solution, lower, pivot_inv, upper_back, coupling, neighbours,
            counts.reshape(1, LANES), colour.reshape(1, LANES))
    return pl.pallas_call(
        functools.partial(kernel, groups),
        out_shape=pltpu.VMEM((1, BLOCK, LANES), jnp.float32),
        in_specs=[pl.BlockSpec(memory_space=pltpu.HBM)] * 9,
        out_specs=pl.BlockSpec(memory_space=pltpu.VMEM),
        scratch_shapes=[matrix] * 4 + [plane] * 4 + [faces] * 2
        + [pltpu.VMEM((FACES, LANES), jnp.int32), line, line]
        + [pltpu.VMEM((2, 2, BLOCK, LANES), jnp.float32), pltpu.VMEM((2, 3, BLOCK, LANES), jnp.float32), pair]
        + [plane] * 8 + [pair]
        + [dma((8,)), dma((12,)), dma((12,)), dma((2,)), dma((2, 2)), dma((3, 2, 2)), dma((2, 3)), dma((2,)), dma((2,))]
        + [pltpu.SemaphoreType.REGULAR((2,))],
        compiler_params=pltpu.CompilerParams(collective_id=0, has_side_effects=True, vmem_limit_bytes=16 << 20),
    )(*[pltpu.with_memory_space_constraint(a, pltpu.HBM) for a in here])


def solution(mesh):
    placed = (
        P("wall", None, "surf"),
        P("wall", None, "surf"),
        P("wall", None, None, "surf"),
        P("wall", None, None, "surf"),
        P("wall", None, None, "surf"),
        P(None, "wall", None, "surf"),
        P(None, "surf"),
        P("surf"),
        P("surf"),
    )
    return jax.shard_map(
        functools.partial(shards, mesh.shape["surf"]), mesh=mesh, in_specs=placed, out_specs=P("wall", None, "surf"),
        check_vma=False,
    )
```

time: 22 us -> 21.1 us (0.959)
  Pallas kernels: 21.3 us -> 20.4 us
    pallas_call x1, Pallas kernels: 21.3 us -> 20.4 us  [shards(): pl.pallas_call(functools.partial(kernel, groups), out_shape=pltpu.VMEM((1...]
where the time goes in v3:
time: 21.1 us; the launch traced here: 21 us
  Pallas kernels  20.4 us (97%)
  local copies, waits for them, and re-layouts  0.62 us (3%)
    pallas_call x1, Pallas kernels, shards(): pl.pallas_call(functools.partial(kernel, groups), out_shape=pltpu.VMEM((1...  20.4 us
    unnamed x1, local copies, waits for them, and re-layouts  0.62 us

profile of v3, /device:TPU:1, one launch (start us, length us, event | category | flops | bytes accessed | tf_op | source)
XLA Modules:
  0.0 21.0 jit_solution(11944248010683637013)
XLA Ops:
  0.0 20.4 %shard_map.91 = f32[1,64,128]{2,1,0:T(8,128)S(1)} custom-call(f32[1,64,128]{2,1,0:T(8,128)} %rhs.1, f32[1,64,128]{2,1,0:T(8,128)} %prev.1, f32[1,64,64,128]{3,2,1,0:T(8,128)} %lower.1, f32[1,64,64,128]{3,2,1,0:T(8,128)} %pivot.1, f32[1,64,64,128]{3,2,1,0:T(8,128)} %upper.1, f32[4,1,64,128]{3,2,1,0:T(8,128)} %coupling.1, s32[4,128]{1,0:T(4,128)} %neighbours.1, ...), custom_call_target="tpu_custom_call" | custom-call | tf_op jit(solution)/shard_map/pallas_call | solution.py:415
  20.4 0.6 %copy.11 = f32[1,64,128]{2,1,0:T(8,128)} copy(f32[1,64,128]{2,1,0:T(8,128)S(1)} %shard_map.91) | data formatting | bytes 65536

commit v4 on v3

--- a/solution.py
+++ b/solution.py
@@ -13,6 +13,7 @@
 LANES = 128
 SUB = 8
 TILES = BLOCK // SUB
+HALVES = {0: pl.ds(0, BLOCK // 2), 3: pl.ds(BLOCK // 2, BLOCK // 2)}
 ROW = 4
 PLANE = 16
 
@@ -39,7 +40,7 @@
     return terms[0]
 
 
-def products(pairs, finish, masks):
+def products(pairs, finish, masks, first=0, last=TILES):
     vecs = [[vec[pl.ds(SUB * b, SUB), :] for b in range(TILES)] for _, vec in pairs]
 
     def body(j, _):
@@ -53,11 +54,11 @@
         finish(j, fold(parts, masks))
         return 0
 
-    lax.fori_loop(0, TILES, body, 0, unroll=TILES)
+    lax.fori_loop(first, last, body, 0, unroll=last - first)
 
 
 def kernel(groups, rhs, prev, lower, pivot, upper, coupling, neighbours, counts, colour, out,
-           mat_l, mat_p1, mat_p0, mat_u, v0, v1, r0, r1, c0, c1, nb, cnt, col, h1, h2, f0, f1, x1, cur0, cur1, part_t, part_u,
+           mat_l, mat_p1, mat_p0, mat_u, v0, v1, r0, r1, c0, c1, nb, cnt, col, h1, h2, f0, f1, x1, cur0, cur1, part_t, part_u, early,
            got_y, got_x, hop, loc, wsend, wrecv, s1, q1, s2, q2, rsend, rrecv, ready):
     s = lax.axis_index("surf")
     w = lax.axis_index("wall")
@@ -89,12 +90,21 @@
             device_id=(right if side == 0 else left, 1), device_id_type=MESH)
 
     def again_copy(src, kind, side, core):
+        dst = h2.at[side, kind % 3]
+        if kind in HALVES:
+            src, dst = src.at[HALVES[kind]], dst.at[HALVES[kind]]
         return pltpu.make_async_remote_copy(
-            src_ref=src, dst_ref=h2.at[side, kind], send_sem=s2.at[kind, side, core], recv_sem=q2.at[side, kind],
+            src_ref=src, dst_ref=dst, send_sem=s2.at[kind, side, core], recv_sem=q2.at[side, kind],
             device_id=(right if side == 0 else left, core), device_id_type=MESH)
 
-    def again_copies(src, kind, core):
-        return [again_copy(src, kind, side, core) for side in (0, 1)]
+    def again_copies(src, kind):
+        return [again_copy(src, kind, side, 1) for side in (0, 1)]
+
+    def twin(src, kind, act):
+        for source, side in ((last_line, 0), (1, 1)):
+            @pl.when(s == source)
+            def _():
+                act(again_copy(src, kind, side, 0))
 
     down = [wall_copy(prev.at[0], v0, 0, 1), wall_copy(rhs.at[0], r0, 1, 1), wall_copy(coupling.at[:, 0], c0, 2, 1),
             wall_copy(upper.at[0], mat_u, 3, 1)]
@@ -102,8 +112,9 @@
     up = [wall_copy(rhs.at[0], r1, 5, 0), wall_copy(coupling.at[:, 0], c1, 6, 0), wall_copy(lower.at[0], mat_l, 7, 0),
           wall_copy(pivot.at[0], mat_p1, 8, 0)]
     up_cur = wall_copy(cur1, cur1, 9, 0)
-    up_y = wall_copy(f0.at[0], got_y, 10, 0)
-    up_x = wall_copy(x1, got_x, 11, 0)
+    up_early = wall_copy(early, got_y.at[0], 10, 0)
+    up_y = [wall_copy(f0.at[i], got_y.at[i], 10 + i, 0) for i in (0, 1)]
+    up_x = [wall_copy(x1.at[i], got_x.at[i], 12 + i, 0) for i in (0, 1)]
 
     def start_slow_first(copies):
         @pl.when(place == 0)
@@ -119,9 +130,13 @@
     def send_prev(row, copies):
         copies[0].start()
 
-        @pl.when((s != 0) & ((s != last_line) | (row == 0)))
+        @pl.when((s != 0) & (s != last_line))
         def _():
             copies[1].start()
+
+    def send_prev_late(copies):
+        pl.semaphore_wait(ready.at[1], 1)
+        copies[1].start()
 
     step1, step2 = ROW - 1, PLANE - 1
 
@@ -132,6 +147,9 @@
     start = [relay(prev.at[0], hop.at[row], row, step1, rrecv.at[row]) for row in (0, 1)]
     middle = [relay(hop.at[row], hop.at[row], row, step2, rrecv.at[row]) for row in (0, 1)]
     end = [relay(hop.at[row], h1.at[1, row], row, last_line, q1.at[1, row]) for row in (0, 1)]
+    end_twin = pltpu.make_async_remote_copy(
+        src_ref=hop.at[0], dst_ref=h1.at[1, 0], send_sem=rsend.at[2], recv_sem=q1.at[1, 0], device_id=(last_line, 0),
+        device_id_type=MESH)
 
     def finish_sends(first, others):
         for c in [first[0]] + others:
@@ -141,8 +159,11 @@
         def _():
             first[1].wait_send()
 
-    def arrived(buf, recv, side, kind):
-        pltpu.make_async_copy(buf.at[side, kind], buf.at[side, kind], recv.at[side, kind]).wait()
+    def arrived(buf, recv, side, kind, half=None):
+        ref = buf.at[side, kind % 3]
+        if half is not None:
+            ref = ref.at[half]
+        pltpu.make_async_copy(ref, ref, recv.at[side, kind]).wait()
 
     def make_solver():
         owners = ([], [], [])
@@ -172,22 +193,37 @@
 
             lax.fori_loop(0, TILES, body, 0, unroll=TILES)
 
-        def take(total, buf, recv, side, kind, held_by, row, sign, scale=None):
-            arrived(buf, recv, side, kind)
+        def take(total, buf, recv, side, kind, held_by, row, sign, scale=None, half=None):
+            arrived(buf, recv, side, kind, half)
 
             def body(j, _):
-                value = minus(total[tile(j), :], row, j, buf[side, kind, tile(j), :], held_by, sign)
+                value = minus(total[tile(j), :], row, j, buf[side, kind % 3, tile(j), :], held_by, sign)
                 total[tile(j), :] = value if scale is None else scale * value
                 return 0
 
-            lax.fori_loop(0, TILES, body, 0, unroll=TILES)
-
-        def solve_first(after_y, finish):
+            begin = 0 if half is None else half.start // SUB
+            count = TILES if half is None else half.size // SUB
+            lax.fori_loop(begin, begin + count, body, 0, unroll=count)
+
+        def far_first(total):
+            take(total, h1, q1, slow, 0, far, 0, -1, alive[0])
+
+        def solve_first(finish):
             y0 = f0.at[0]
+            take(y0, h1, q1, quick, 0, near, 0, -1)
+
+            @pl.when(s == last_line)
+            def _():
+                early[...] = y0[...]
+                up_early.start()
+
             take(f1, h1, q1, quick, 1, near, 1, -1)
-            take(y0, h1, q1, quick, 0, near, 0, -1)
-            take(y0, h1, q1, slow, 0, far, 0, -1, alive[0])
-            after_y()
+            far_first(y0)
+
+            @pl.when(s != last_line)
+            def _():
+                up_y[0].start()
+
             arrived(h1, q1, slow, 1)
 
             def forward(j, t):
@@ -197,12 +233,14 @@
             products([(mat_l, y0)], forward, masks)
             products([(mat_p1, f1)], finish, masks)
 
-        def solve_second(finish):
+        def solve_second(after_y, finish):
             y0 = f0.at[1]
             for side, held_by in ((quick, near), (slow, far)):
                 take(f1, h2, q2, side, 2, held_by, 1, -1)
                 take(y0, h2, q2, side, 1, held_by, 0, 1)
-                take(y0, h2, q2, side, 0, held_by, 0, -1, alive[0] if held_by is far else None)
+                for kind, half in HALVES.items():
+                    take(y0, h2, q2, side, kind, held_by, 0, -1, alive[0] if held_by is far else None, half)
+            after_y()
 
             def forward(j, t):
                 f1[tile(j), :] = alive[1] * (f1[tile(j), :] - t)
@@ -210,7 +248,7 @@
             products([(mat_l, y0)], forward, masks)
             products([(mat_p1, f1)], finish, masks)
 
-        return own_part, solve_first, solve_second, alive, colours
+        return own_part, far_first, solve_first, solve_second, alive, colours
 
     @pl.when(w == 0)
     def _():
@@ -223,15 +261,24 @@
         def _():
             start[0].start()
 
+        @pl.when(s == last_line)
+        def _():
+            signal(ready.at[2], step2, 1)
+
         first = [first_copy(side, 0) for side in (0, 1)]
         send_prev(0, first)
         for c in down:
             c.start()
         for c in mine:
             c.start()
+
+        @pl.when(s == last_line)
+        def _():
+            send_prev_late(first)
+
         for c in mine:
             c.wait()
-        own_part, solve_first, solve_second, alive, colours = make_solver()
+        own_part, far_first, solve_first, solve_second, alive, colours = make_solver()
 
         def term(j, t):
             part_t[tile(j), :] = jnp.where(colours == 0, alive[0] * t, v0[tile(j), :])
@@ -239,35 +286,57 @@
         def first0(j, t):
             cur0[tile(j), :] = part_t[tile(j), :] - jnp.where(colours == 0, alive[0] * t, 0.0)
 
-        def second1(j, t):
-            x1[tile(j), :] = alive[1] * t
-
-        def second0(j, t):
+        def keep(j, t):
+            part_u[tile(j), :] = t
+
+        def result(j, t):
             out[0, tile(j), :] = jnp.where(colours == 1, alive[0] * t, cur0[tile(j), :])
 
-        up_y.wait_recv()
-        products([(mat_p0, got_y)], term, masks)
-        again = [again_copies(part_t, 0, core) for core in (1, 0)]
-        start_slow_first(again[0])
+        up_y[0].wait_recv()
+
+        @pl.when(s == last_line)
+        def _():
+            far_first(got_y.at[0])
+
+        again = []
+        for kind, half in HALVES.items():
+            begin = half.start // SUB
+            products([(mat_p0, got_y.at[0])], term, masks, begin, begin + half.size // SUB)
+            copies = again_copies(part_t, kind)
+            start_slow_first(copies)
+            again += copies
         down_t.start()
-        start_slow_first(again[1])
-        up_x.wait_recv()
-        products([(mat_u, got_x)], first0, masks)
-        up[0].wait_recv()
-        up[1].wait_recv()
-        own_part(f0.at[1], r0, 0, cur0)
-        up_cur.wait_recv()
-        own_part(f1, r1, 1, cur1)
-        up[2].wait_recv()
-        up[3].wait_recv()
-        solve_second(second1)
-        products([(mat_p0, f0.at[1]), (mat_u, x1)], second0, masks)
-        finish_sends(first, again[0] + again[1] + down + [down_t])
-
-        @pl.when(s == 0)
-        def _():
+        for kind in HALVES:
+            twin(part_t, kind, lambda c: c.start())
+        up_x[0].wait_recv()
+        products([(mat_u, got_x.at[0])], first0, masks)
+
+        @pl.when(s == 0)
+        def _():
+            def second1(j, t):
+                x1[1, tile(j), :] = alive[1] * t
+
+            up[0].wait_recv()
+            up[1].wait_recv()
+            own_part(f0.at[1], r0, 0, cur0)
+            up_cur.wait_recv()
+            own_part(f1, r1, 1, cur1)
+            up[2].wait_recv()
+            up[3].wait_recv()
+            solve_second(lambda: None, second1)
+            products([(mat_p0, f0.at[1]), (mat_u, x1.at[1])], result, masks)
             start[0].wait_send()
 
+        @pl.when(s != 0)
+        def _():
+            up_y[1].wait_recv()
+            products([(mat_p0, got_y.at[1])], keep, masks)
+            up_x[1].wait_recv()
+            products([(mat_u, got_x.at[1])], lambda j, t: result(j, part_u[tile(j), :] - t), masks)
+
+        for kind in HALVES:
+            twin(part_t, kind, lambda c: c.wait_send())
+        finish_sends(first, again + down + [down_t])
 
     @pl.when(w == 1)
     def _():
@@ -278,12 +347,9 @@
         greet(left, 0)
         greet(left, 1)
 
-        @pl.when(s != last_line)
+        @pl.when(s < last_line - 1)
         def _():
             greet(right, 0)
-
-        @pl.when(s < last_line - 1)
-        def _():
             greet(right, 1)
 
         @pl.when(s == step1)
@@ -294,6 +360,7 @@
 
         @pl.when(s == step2)
         def _():
+            greet(last_line, 0)
             greet(last_line, 1)
 
         mine = [local(prev.at[0], v1, 0), local(rhs.at[0], r1, 1), local(coupling.at[:, 0], c1, 2),
@@ -325,8 +392,7 @@
 
         @pl.when(s == last_line)
         def _():
-            pl.semaphore_wait(ready.at[1], 1)
-            first[1].start()
+            send_prev_late(first)
 
         def pass_on(arriving, leaving):
             pl.semaphore_wait(ready.at[0], 1)
@@ -341,43 +407,56 @@
         @pl.when(s == step2)
         def _():
             pass_on(middle, end)
+            pl.semaphore_wait(ready.at[2], 1)
+            end_twin.start()
 
         for c in mine[:6]:
             c.wait()
-        own_part, solve_first, solve_second, alive, colours = make_solver()
+        own_part, far_first, solve_first, solve_second, alive, colours = make_solver()
         own_part(f1, r1, 1, v1)
         for c in down[:3]:
             c.wait_recv()
-        for c in up[:3]:
-            c.start()
+
+        @pl.when(s == last_line)
+        def _():
+            signal(ready.at[1], last_line, 0)
+
+        @pl.when(s == 0)
+        def _():
+            for c in up:
+                c.start()
+
         own_part(f0.at[0], r0, 0, v0)
         mine[6].wait()
         mine[7].wait()
 
         def first1(j, t):
-            x1[tile(j), :] = alive[1] * t
+            x1[0, tile(j), :] = alive[1] * t
             cur1[tile(j), :] = jnp.where(colours == 0, alive[1] * t, v1[tile(j), :])
 
         def term(j, t):
             part_u[tile(j), :] = jnp.where(colours == 0, alive[0] * t, 0.0)
 
         def second1(j, t):
+            x1[1, tile(j), :] = alive[1] * t
             out[0, tile(j), :] = jnp.where(colours == 1, alive[1] * t, cur1[tile(j), :])
 
-        solve_first(up_y.start, first1)
-        again1 = [again_copies(cur1, 2, core) for core in (1, 0)]
-        start_slow_first(again1[0])
+        solve_first(first1)
+        again1 = again_copies(cur1, 2)
+        start_slow_first(again1)
         down[3].wait_recv()
-        products([(mat_u, x1)], term, masks)
-        again0 = [again_copies(part_u, 1, core) for core in (1, 0)]
-        start_slow_first(again0[0])
-        up_x.start()
-        up_cur.start()
-        start_slow_first(again0[1])
-        start_slow_first(again1[1])
-        up[3].start()
+        products([(mat_u, x1.at[0])], term, masks)
+        again0 = again_copies(part_u, 1)
+        start_slow_first(again0)
+        up_x[0].start()
         own_part(f1, r1, 1, cur1)
         down_t.wait_recv()
+        twin(cur1, 2, lambda c: c.start())
+        twin(part_u, 1, lambda c: c.start())
+
+        @pl.when(s == 0)
+        def _():
+            up_cur.start()
 
         def join(j, _):
             cur0[tile(j), :] = part_t[tile(j), :] - part_u[tile(j), :]
@@ -385,8 +464,31 @@
 
         lax.fori_loop(0, TILES, join, 0, unroll=TILES)
         own_part(f0.at[1], r0, 0, cur0)
-        solve_second(second1)
-        finish_sends(first, up + [up_cur, up_y, up_x] + again0[0] + again0[1] + again1[0] + again1[1])
+
+        def after_y():
+            @pl.when(s != 0)
+            def _():
+                up_y[1].start()
+
+        solve_second(after_y, second1)
+
+        @pl.when(s != 0)
+        def _():
+            up_x[1].start()
+
+        twin(cur1, 2, lambda c: c.wait_send())
+        twin(part_u, 1, lambda c: c.wait_send())
+        finish_sends(first, [up_y[0], up_x[0]] + again0 + again1)
+
+        @pl.when(s != 0)
+        def _():
+            up_y[1].wait_send()
+            up_x[1].wait_send()
+
+        @pl.when(s == 0)
+        def _():
+            for c in up + [up_cur]:
+                c.wait_send()
 
         @pl.when(s == 0)
         def _():
@@ -399,7 +501,7 @@
 
         @pl.when(s == step2)
         def _():
-            for c in end:
+            for c in end + [end_twin]:
                 c.wait_send()
 
 
@@ -420,9 +522,9 @@
         scratch_shapes=[matrix] * 4 + [plane] * 4 + [faces] * 2
         + [pltpu.VMEM((FACES, LANES), jnp.int32), line, line]
         + [pltpu.VMEM((2, 2, BLOCK, LANES), jnp.float32), pltpu.VMEM((2, 3, BLOCK, LANES), jnp.float32), pair]
-        + [plane] * 8 + [pair]
-        + [dma((8,)), dma((12,)), dma((12,)), dma((2,)), dma((2, 2)), dma((3, 2, 2)), dma((2, 3)), dma((2,)), dma((2,))]
-        + [pltpu.SemaphoreType.REGULAR((2,))],
+        + [plane, pair] + [plane] * 5 + [pair] * 3
+        + [dma((8,)), dma((14,)), dma((14,)), dma((2,)), dma((2, 2)), dma((4, 2, 2)), dma((2, 4)), dma((3,)), dma((2,))]
+        + [pltpu.SemaphoreType.REGULAR((3,))],
         compiler_params=pltpu.CompilerParams(collective_id=0, has_side_effects=True, vmem_limit_bytes=16 << 20),
     )(*[pltpu.with_memory_space_constraint(a, pltpu.HBM) for a in here])
 

time: 21.1 us -> 20.4 us (0.967)
  Pallas kernels: 20.4 us -> 19.7 us
    pallas_call x1, Pallas kernels: 20.4 us -> 19.7 us  [shards(): pl.pallas_call(functools.partial(kernel, groups), out_shape=pltpu.VMEM((1...]
where the time goes in v4:
time: 20.4 us; the launch traced here: 20.3 us
  Pallas kernels  19.7 us (97%)
  local copies, waits for them, and re-layouts  0.62 us (3%)
    pallas_call x1, Pallas kernels, shards(): pl.pallas_call(functools.partial(kernel, groups), out_shape=pltpu.VMEM((1...  19.7 us
    unnamed x1, local copies, waits for them, and re-layouts  0.62 us

profile of v4, /device:TPU:1, one launch (start us, length us, event | category | flops | bytes accessed | tf_op | source)
XLA Modules:
  0.0 20.3 jit_solution(5019576438150076171)
XLA Ops:
  0.0 19.7 %shard_map.91 = f32[1,64,128]{2,1,0:T(8,128)S(1)} custom-call(f32[1,64,128]{2,1,0:T(8,128)} %rhs.1, f32[1,64,128]{2,1,0:T(8,128)} %prev.1, f32[1,64,64,128]{3,2,1,0:T(8,128)} %lower.1, f32[1,64,64,128]{3,2,1,0:T(8,128)} %pivot.1, f32[1,64,64,128]{3,2,1,0:T(8,128)} %upper.1, f32[4,1,64,128]{3,2,1,0:T(8,128)} %coupling.1, s32[4,128]{1,0:T(4,128)} %neighbours.1, ...), custom_call_target="tpu_custom_call" | custom-call | tf_op jit(solution)/shard_map/pallas_call | solution.py:517
  19.7 0.6 %copy.11 = f32[1,64,128]{2,1,0:T(8,128)} copy(f32[1,64,128]{2,1,0:T(8,128)S(1)} %shard_map.91) | data formatting | bytes 65536

commit v5 on v4

--- a/solution.py
+++ b/solution.py
@@ -113,7 +113,10 @@
           wall_copy(pivot.at[0], mat_p1, 8, 0)]
     up_cur = wall_copy(cur1, cur1, 9, 0)
     up_early = wall_copy(early, got_y.at[0], 10, 0)
-    up_y = [wall_copy(f0.at[i], got_y.at[i], 10 + i, 0) for i in (0, 1)]
+    up_y = wall_copy(f0.at[1], got_y.at[1], 11, 0)
+    up_far = pltpu.make_async_remote_copy(
+        src_ref=h1.at[slow, 0], dst_ref=h1.at[slow, 0], send_sem=wsend.at[14], recv_sem=q1.at[slow, 0], device_id=(s, 0),
+        device_id_type=MESH)
     up_x = [wall_copy(x1.at[i], got_x.at[i], 12 + i, 0) for i in (0, 1)]
 
     def start_slow_first(copies):
@@ -147,9 +150,6 @@
     start = [relay(prev.at[0], hop.at[row], row, step1, rrecv.at[row]) for row in (0, 1)]
     middle = [relay(hop.at[row], hop.at[row], row, step2, rrecv.at[row]) for row in (0, 1)]
     end = [relay(hop.at[row], h1.at[1, row], row, last_line, q1.at[1, row]) for row in (0, 1)]
-    end_twin = pltpu.make_async_remote_copy(
-        src_ref=hop.at[0], dst_ref=h1.at[1, 0], send_sem=rsend.at[2], recv_sem=q1.at[1, 0], device_id=(last_line, 0),
-        device_id_type=MESH)
 
     def finish_sends(first, others):
         for c in [first[0]] + others:
@@ -206,24 +206,21 @@
             lax.fori_loop(begin, begin + count, body, 0, unroll=count)
 
         def far_first(total):
-            take(total, h1, q1, slow, 0, far, 0, -1, alive[0])
+            def body(j, _):
+                total[tile(j), :] = alive[0] * minus(total[tile(j), :], 0, j, h1[slow, 0, tile(j), :], far, -1)
+                return 0
+
+            lax.fori_loop(0, TILES, body, 0, unroll=TILES)
 
         def solve_first(finish):
             y0 = f0.at[0]
             take(y0, h1, q1, quick, 0, near, 0, -1)
-
-            @pl.when(s == last_line)
-            def _():
-                early[...] = y0[...]
-                up_early.start()
-
+            early[...] = y0[...]
+            up_early.start()
             take(f1, h1, q1, quick, 1, near, 1, -1)
+            arrived(h1, q1, slow, 0)
+            up_far.start()
             far_first(y0)
-
-            @pl.when(s != last_line)
-            def _():
-                up_y[0].start()
-
             arrived(h1, q1, slow, 1)
 
             def forward(j, t):
@@ -255,15 +252,11 @@
         mine = [local(prev.at[0], v0, 0), local(rhs.at[0], r0, 1), local(coupling.at[:, 0], c0, 2),
                 local(neighbours, nb, 3), local(counts, cnt, 4), local(colour, col, 5),
                 local(pivot.at[0], mat_p0, 6), local(upper.at[0], mat_u, 7)]
-        pl.semaphore_wait(barrier, 3)
+        pl.semaphore_wait(barrier, jnp.where(s == last_line, 2, 3))
 
         @pl.when(s == 0)
         def _():
             start[0].start()
-
-        @pl.when(s == last_line)
-        def _():
-            signal(ready.at[2], step2, 1)
 
         first = [first_copy(side, 0) for side in (0, 1)]
         send_prev(0, first)
@@ -292,12 +285,9 @@
         def result(j, t):
             out[0, tile(j), :] = jnp.where(colours == 1, alive[0] * t, cur0[tile(j), :])
 
-        up_y[0].wait_recv()
-
-        @pl.when(s == last_line)
-        def _():
-            far_first(got_y.at[0])
-
+        up_early.wait_recv()
+        arrived(h1, q1, slow, 0)
+        far_first(got_y.at[0])
         again = []
         for kind, half in HALVES.items():
             begin = half.start // SUB
@@ -329,7 +319,7 @@
 
         @pl.when(s != 0)
         def _():
-            up_y[1].wait_recv()
+            up_y.wait_recv()
             products([(mat_p0, got_y.at[1])], keep, masks)
             up_x[1].wait_recv()
             products([(mat_u, got_x.at[1])], lambda j, t: result(j, part_u[tile(j), :] - t), masks)
@@ -343,9 +333,14 @@
         def greet(to, core):
             signal(barrier, to, core)
 
-        greet(s, 0)
+        @pl.when(s == last_line)
+        def _():
+            pl.semaphore_wait(barrier, 2)
+            signal(ready.at[0], step2, 1)
+
         greet(left, 0)
         greet(left, 1)
+        greet(s, 0)
 
         @pl.when(s < last_line - 1)
         def _():
@@ -360,18 +355,15 @@
 
         @pl.when(s == step2)
         def _():
-            greet(last_line, 0)
             greet(last_line, 1)
 
         mine = [local(prev.at[0], v1, 0), local(rhs.at[0], r1, 1), local(coupling.at[:, 0], c1, 2),
                 local(neighbours, nb, 3), local(counts, cnt, 4), local(colour, col, 5),
                 local(lower.at[0], mat_l, 6), local(pivot.at[0], mat_p1, 7)]
-        ends = (s == 0) | (s == last_line)
-        pl.semaphore_wait(barrier, jnp.where(ends, 1, 2) + jnp.where(ends | (s == step2), 1, 0))
-
-        @pl.when(s == last_line)
-        def _():
-            signal(ready.at[0], step2, 1)
+
+        @pl.when(s != last_line)
+        def _():
+            pl.semaphore_wait(barrier, jnp.where(s == step2, 3, 2))
 
         @pl.when(s == step2)
         def _():
@@ -407,8 +399,6 @@
         @pl.when(s == step2)
         def _():
             pass_on(middle, end)
-            pl.semaphore_wait(ready.at[2], 1)
-            end_twin.start()
 
         for c in mine[:6]:
             c.wait()
@@ -468,7 +458,7 @@
         def after_y():
             @pl.when(s != 0)
             def _():
-                up_y[1].start()
+                up_y.start()
 
         solve_second(after_y, second1)
 
@@ -478,11 +468,11 @@
 
         twin(cur1, 2, lambda c: c.wait_send())
         twin(part_u, 1, lambda c: c.wait_send())
-        finish_sends(first, [up_y[0], up_x[0]] + again0 + again1)
+        finish_sends(first, [up_early, up_far, up_x[0]] + again0 + again1)
 
         @pl.when(s != 0)
         def _():
-            up_y[1].wait_send()
+            up_y.wait_send()
             up_x[1].wait_send()
 
         @pl.when(s == 0)
@@ -501,7 +491,7 @@
 
         @pl.when(s == step2)
         def _():
-            for c in end + [end_twin]:
+            for c in end:
                 c.wait_send()
 
 
@@ -523,8 +513,8 @@
         + [pltpu.VMEM((FACES, LANES), jnp.int32), line, line]
         + [pltpu.VMEM((2, 2, BLOCK, LANES), jnp.float32), pltpu.VMEM((2, 3, BLOCK, LANES), jnp.float32), pair]
         + [plane, pair] + [plane] * 5 + [pair] * 3
-        + [dma((8,)), dma((14,)), dma((14,)), dma((2,)), dma((2, 2)), dma((4, 2, 2)), dma((2, 4)), dma((3,)), dma((2,))]
-        + [pltpu.SemaphoreType.REGULAR((3,))],
+        + [dma((8,)), dma((15,)), dma((15,)), dma((2,)), dma((2, 2)), dma((4, 2, 2)), dma((2, 4)), dma((2,)), dma((2,))]
+        + [pltpu.SemaphoreType.REGULAR((2,))],
         compiler_params=pltpu.CompilerParams(collective_id=0, has_side_effects=True, vmem_limit_bytes=16 << 20),
     )(*[pltpu.with_memory_space_constraint(a, pltpu.HBM) for a in here])
 

time: 20.4 us -> 20.1 us (0.985)
  Pallas kernels: 19.7 us -> 19.4 us
    pallas_call x1, Pallas kernels: 19.7 us -> 19.4 us  [shards(): pl.pallas_call(functools.partial(kernel, groups), out_shape=pltpu.VMEM((1...]
where the time goes in v5:
time: 20.1 us
  Pallas kernels  19.4 us (97%)
  local copies, waits for them, and re-layouts  0.62 us (3%)
    pallas_call x1, Pallas kernels, shards(): pl.pallas_call(functools.partial(kernel, groups), out_shape=pltpu.VMEM((1...  19.4 us
    unnamed x1, local copies, waits for them, and re-layouts  0.62 us

profile of v5, /device:TPU:1, one launch (start us, length us, event | category | flops | bytes accessed | tf_op | source)
XLA Modules:
  0.0 20.1 jit_solution(5592036484096908984)
XLA Ops:
  0.0 19.4 %shard_map.91 = f32[1,64,128]{2,1,0:T(8,128)S(1)} custom-call(f32[1,64,128]{2,1,0:T(8,128)} %rhs.1, f32[1,64,128]{2,1,0:T(8,128)} %prev.1, f32[1,64,64,128]{3,2,1,0:T(8,128)} %lower.1, f32[1,64,64,128]{3,2,1,0:T(8,128)} %pivot.1, f32[1,64,64,128]{3,2,1,0:T(8,128)} %upper.1, f32[4,1,64,128]{3,2,1,0:T(8,128)} %coupling.1, s32[4,128]{1,0:T(4,128)} %neighbours.1, ...), custom_call_target="tpu_custom_call" | custom-call | tf_op jit(solution)/shard_map/pallas_call | solution.py:507
  19.5 0.6 %copy.11 = f32[1,64,128]{2,1,0:T(8,128)} copy(f32[1,64,128]{2,1,0:T(8,128)S(1)} %shard_map.91) | data formatting | bytes 65536

commit v6 on v5

--- a/solution.py
+++ b/solution.py
@@ -14,6 +14,7 @@
 SUB = 8
 TILES = BLOCK // SUB
 HALVES = {0: pl.ds(0, BLOCK // 2), 3: pl.ds(BLOCK // 2, BLOCK // 2)}
+PARTS = {0: HALVES[0], 2: HALVES[3]}
 ROW = 4
 PLANE = 16
 
@@ -84,10 +85,13 @@
         return pltpu.make_async_remote_copy(src_ref=src, dst_ref=dst, send_sem=wsend.at[i], recv_sem=wrecv.at[i],
                                             device_id=(s, to), device_id_type=MESH)
 
-    def first_copy(side, row):
-        return pltpu.make_async_remote_copy(
-            src_ref=prev.at[0], dst_ref=h1.at[side, row], send_sem=s1.at[side], recv_sem=q1.at[side, row],
-            device_id=(right if side == 0 else left, 1), device_id_type=MESH)
+    def piece(ref, part):
+        return ref if part == 1 else ref.at[PARTS[part]]
+
+    def first_copies(side, parts):
+        return [pltpu.make_async_remote_copy(
+            src_ref=piece(prev.at[0], part), dst_ref=piece(h1.at[side, part % 2], part), send_sem=s1.at[side, part],
+            recv_sem=q1.at[side, part], device_id=(right if side == 0 else left, 1), device_id_type=MESH) for part in parts]
 
     def again_copy(src, kind, side, core):
         dst = h2.at[side, kind % 3]
@@ -114,9 +118,9 @@
     up_cur = wall_copy(cur1, cur1, 9, 0)
     up_early = wall_copy(early, got_y.at[0], 10, 0)
     up_y = wall_copy(f0.at[1], got_y.at[1], 11, 0)
-    up_far = pltpu.make_async_remote_copy(
-        src_ref=h1.at[slow, 0], dst_ref=h1.at[slow, 0], send_sem=wsend.at[14], recv_sem=q1.at[slow, 0], device_id=(s, 0),
-        device_id_type=MESH)
+    up_far = {part: pltpu.make_async_remote_copy(
+        src_ref=piece(h1.at[slow, 0], part), dst_ref=piece(h1.at[slow, 0], part), send_sem=wsend.at[14 + part // 2],
+        recv_sem=q1.at[slow, part], device_id=(s, 0), device_id_type=MESH) for part in PARTS}
     up_x = [wall_copy(x1.at[i], got_x.at[i], 12 + i, 0) for i in (0, 1)]
 
     def start_slow_first(copies):
@@ -130,34 +134,45 @@
             copies[0].start()
             copies[1].start()
 
-    def send_prev(row, copies):
-        copies[0].start()
+    def start_all(copies):
+        for c in copies:
+            c.start()
+
+    def send_prev(copies):
+        start_all(copies[0])
 
         @pl.when((s != 0) & (s != last_line))
         def _():
-            copies[1].start()
+            start_all(copies[1])
 
     def send_prev_late(copies):
         pl.semaphore_wait(ready.at[1], 1)
-        copies[1].start()
+        start_all(copies[1])
 
     step1, step2 = ROW - 1, PLANE - 1
 
-    def relay(src, dst, row, to, recv):
+    def relay(src, dst, part, to, recv):
         return pltpu.make_async_remote_copy(
-            src_ref=src, dst_ref=dst, send_sem=rsend.at[row], recv_sem=recv, device_id=(to, 1), device_id_type=MESH)
-
-    start = [relay(prev.at[0], hop.at[row], row, step1, rrecv.at[row]) for row in (0, 1)]
-    middle = [relay(hop.at[row], hop.at[row], row, step2, rrecv.at[row]) for row in (0, 1)]
-    end = [relay(hop.at[row], h1.at[1, row], row, last_line, q1.at[1, row]) for row in (0, 1)]
+            src_ref=piece(src, part), dst_ref=piece(dst, part), send_sem=rsend.at[part], recv_sem=recv, device_id=(to, 1),
+            device_id_type=MESH)
+
+    order = (0, 2, 1)
+    start = {part: relay(prev.at[0], hop.at[part % 2], part, step1, rrecv.at[part]) for part in order}
+    middle = {part: relay(hop.at[part % 2], hop.at[part % 2], part, step2, rrecv.at[part]) for part in order}
+    end = {part: relay(hop.at[part % 2], h1.at[1, part % 2], part, last_line, q1.at[1, part]) for part in order}
 
     def finish_sends(first, others):
-        for c in [first[0]] + others:
+        for c in first[0] + others:
             c.wait_send()
 
         @pl.when(s != 0)
         def _():
-            first[1].wait_send()
+            for c in first[1]:
+                c.wait_send()
+
+    def landed(side, part):
+        ref = piece(h1.at[side, part % 2], part)
+        pltpu.make_async_copy(ref, ref, q1.at[side, part]).wait()
 
     def arrived(buf, recv, side, kind, half=None):
         ref = buf.at[side, kind % 3]
@@ -205,23 +220,35 @@
             count = TILES if half is None else half.size // SUB
             lax.fori_loop(begin, begin + count, body, 0, unroll=count)
 
-        def far_first(total):
+        def take_first(total, side, held_by, part, scale=None):
+            row = part % 2
+
             def body(j, _):
-                total[tile(j), :] = alive[0] * minus(total[tile(j), :], 0, j, h1[slow, 0, tile(j), :], far, -1)
+                value = minus(total[tile(j), :], row, j, h1[side, row, tile(j), :], held_by, -1)
+                total[tile(j), :] = value if scale is None else scale * value
                 return 0
 
-            lax.fori_loop(0, TILES, body, 0, unroll=TILES)
+            begin = 0 if part == 1 else PARTS[part].start // SUB
+            count = TILES if part == 1 else PARTS[part].size // SUB
+            lax.fori_loop(begin, begin + count, body, 0, unroll=count)
+
+        def far_first(total, part):
+            take_first(total, slow, far, part, alive[0])
 
         def solve_first(finish):
             y0 = f0.at[0]
-            take(y0, h1, q1, quick, 0, near, 0, -1)
+            for part in PARTS:
+                landed(quick, part)
+                take_first(y0, quick, near, part)
             early[...] = y0[...]
             up_early.start()
-            take(f1, h1, q1, quick, 1, near, 1, -1)
-            arrived(h1, q1, slow, 0)
-            up_far.start()
-            far_first(y0)
-            arrived(h1, q1, slow, 1)
+            landed(quick, 1)
+            take_first(f1, quick, near, 1)
+            for part in PARTS:
+                landed(slow, part)
+                up_far[part].start()
+                far_first(y0, part)
+            landed(slow, 1)
 
             def forward(j, t):
                 source = minus(f1[tile(j), :], 1, j, h1[slow, 1, tile(j), :], far, -1)
@@ -257,9 +284,10 @@
         @pl.when(s == 0)
         def _():
             start[0].start()
-
-        first = [first_copy(side, 0) for side in (0, 1)]
-        send_prev(0, first)
+            start[2].start()
+
+        first = [first_copies(side, (0, 2)) for side in (0, 1)]
+        send_prev(first)
         for c in down:
             c.start()
         for c in mine:
@@ -286,8 +314,9 @@
             out[0, tile(j), :] = jnp.where(colours == 1, alive[0] * t, cur0[tile(j), :])
 
         up_early.wait_recv()
-        arrived(h1, q1, slow, 0)
-        far_first(got_y.at[0])
+        for part in PARTS:
+            landed(slow, part)
+            far_first(got_y.at[0], part)
         again = []
         for kind, half in HALVES.items():
             begin = half.start // SUB
@@ -301,6 +330,10 @@
         up_x[0].wait_recv()
         products([(mat_u, got_x.at[0])], first0, masks)
 
+        for kind in HALVES:
+            twin(part_t, kind, lambda c: c.wait_send())
+        finish_sends(first, again + down + [down_t])
+
         @pl.when(s == 0)
         def _():
             def second1(j, t):
@@ -316,6 +349,7 @@
             solve_second(lambda: None, second1)
             products([(mat_p0, f0.at[1]), (mat_u, x1.at[1])], result, masks)
             start[0].wait_send()
+            start[2].wait_send()
 
         @pl.when(s != 0)
         def _():
@@ -324,10 +358,6 @@
             up_x[1].wait_recv()
             products([(mat_u, got_x.at[1])], lambda j, t: result(j, part_u[tile(j), :] - t), masks)
 
-        for kind in HALVES:
-            twin(part_t, kind, lambda c: c.wait_send())
-        finish_sends(first, again + down + [down_t])
-
     @pl.when(w == 1)
     def _():
         def greet(to, core):
@@ -338,6 +368,16 @@
             pl.semaphore_wait(barrier, 2)
             signal(ready.at[0], step2, 1)
 
+        @pl.when(s == step1)
+        def _():
+            greet(0, 0)
+            greet(0, 1)
+            greet(step2, 1)
+
+        @pl.when(s == step2)
+        def _():
+            greet(last_line, 1)
+
         greet(left, 0)
         greet(left, 1)
         greet(s, 0)
@@ -347,16 +387,6 @@
             greet(right, 0)
             greet(right, 1)
 
-        @pl.when(s == step1)
-        def _():
-            greet(0, 0)
-            greet(0, 1)
-            greet(step2, 1)
-
-        @pl.when(s == step2)
-        def _():
-            greet(last_line, 1)
-
         mine = [local(prev.at[0], v1, 0), local(rhs.at[0], r1, 1), local(coupling.at[:, 0], c1, 2),
                 local(neighbours, nb, 3), local(counts, cnt, 4), local(colour, col, 5),
                 local(lower.at[0], mat_l, 6), local(pivot.at[0], mat_p1, 7)]
@@ -377,8 +407,8 @@
         def _():
             start[1].start()
 
-        first = [first_copy(side, 1) for side in (0, 1)]
-        send_prev(1, first)
+        first = [first_copies(side, (1,)) for side in (0, 1)]
+        send_prev(first)
         for c in mine:
             c.start()
 
@@ -388,9 +418,9 @@
 
         def pass_on(arriving, leaving):
             pl.semaphore_wait(ready.at[0], 1)
-            for row in (0, 1):
-                arriving[row].wait_recv()
-                leaving[row].start()
+            for part in order:
+                arriving[part].wait_recv()
+                leaving[part].start()
 
         @pl.when(s == step1)
         def _():
@@ -455,6 +485,29 @@
         lax.fori_loop(0, TILES, join, 0, unroll=TILES)
         own_part(f0.at[1], r0, 0, cur0)
 
+        twin(cur1, 2, lambda c: c.wait_send())
+        twin(part_u, 1, lambda c: c.wait_send())
+        finish_sends(first, [up_early, up_far[0], up_far[2], up_x[0]] + again0 + again1)
+
+        @pl.when(s == 0)
+        def _():
+            for c in up + [up_cur]:
+                c.wait_send()
+
+        @pl.when(s == 0)
+        def _():
+            start[1].wait_send()
+
+        @pl.when(s == step1)
+        def _():
+            for c in middle.values():
+                c.wait_send()
+
+        @pl.when(s == step2)
+        def _():
+            for c in end.values():
+                c.wait_send()
+
         def after_y():
             @pl.when(s != 0)
             def _():
@@ -466,33 +519,10 @@
         def _():
             up_x[1].start()
 
-        twin(cur1, 2, lambda c: c.wait_send())
-        twin(part_u, 1, lambda c: c.wait_send())
-        finish_sends(first, [up_early, up_far, up_x[0]] + again0 + again1)
-
         @pl.when(s != 0)
         def _():
             up_y.wait_send()
             up_x[1].wait_send()
-
-        @pl.when(s == 0)
-        def _():
-            for c in up + [up_cur]:
-                c.wait_send()
-
-        @pl.when(s == 0)
-        def _():
-            start[1].wait_send()
-
-        @pl.when(s == step1)
-        def _():
-            for c in middle:
-                c.wait_send()
-
-        @pl.when(s == step2)
-        def _():
-            for c in end:
-                c.wait_send()
 
 
 def shards(groups, rhs, prev_solution, lower, pivot_inv, upper_back, coupling, neighbours, counts, colour):
@@ -513,7 +543,7 @@
         + [pltpu.VMEM((FACES, LANES), jnp.int32), line, line]
         + [pltpu.VMEM((2, 2, BLOCK, LANES), jnp.float32), pltpu.VMEM((2, 3, BLOCK, LANES), jnp.float32), pair]
         + [plane, pair] + [plane] * 5 + [pair] * 3
-        + [dma((8,)), dma((15,)), dma((15,)), dma((2,)), dma((2, 2)), dma((4, 2, 2)), dma((2, 4)), dma((2,)), dma((2,))]
+        + [dma((8,)), dma((16,)), dma((14,)), dma((2, 3)), dma((2, 3)), dma((4, 2, 2)), dma((2, 4)), dma((3,)), dma((3,))]
         + [pltpu.SemaphoreType.REGULAR((2,))],
         compiler_params=pltpu.CompilerParams(collective_id=0, has_side_effects=True, vmem_limit_bytes=16 << 20),
     )(*[pltpu.with_memory_space_constraint(a, pltpu.HBM) for a in here])

time: 20.1 us -> 19.8 us (0.985)
    pallas_call x1, Pallas kernels: 19.4 us -> 19.2 us  [shards(): pl.pallas_call(functools.partial(kernel, groups), out_shape=pltpu.VMEM((1...]
where the time goes in v6:
time: 19.8 us
  Pallas kernels  19.2 us (97%)
  local copies, waits for them, and re-layouts  0.62 us (3%)
    pallas_call x1, Pallas kernels, shards(): pl.pallas_call(functools.partial(kernel, groups), out_shape=pltpu.VMEM((1...  19.2 us
    unnamed x1, local copies, waits for them, and re-layouts  0.62 us

profile of v6, /device:TPU:1, one launch (start us, length us, event | category | flops | bytes accessed | tf_op | source)
XLA Modules:
  0.0 19.8 jit_solution(1161014075207677696)
XLA Ops:
  0.0 19.2 %shard_map.91 = f32[1,64,128]{2,1,0:T(8,128)S(1)} custom-call(f32[1,64,128]{2,1,0:T(8,128)} %rhs.1, f32[1,64,128]{2,1,0:T(8,128)} %prev.1, f32[1,64,64,128]{3,2,1,0:T(8,128)} %lower.1, f32[1,64,64,128]{3,2,1,0:T(8,128)} %pivot.1, f32[1,64,64,128]{3,2,1,0:T(8,128)} %upper.1, f32[4,1,64,128]{3,2,1,0:T(8,128)} %coupling.1, s32[4,128]{1,0:T(4,128)} %neighbours.1, ...), custom_call_target="tpu_custom_call" | custom-call | tf_op jit(solution)/shard_map/pallas_call | solution.py:537
  19.2 0.6 %copy.11 = f32[1,64,128]{2,1,0:T(8,128)} copy(f32[1,64,128]{2,1,0:T(8,128)S(1)} %shard_map.91) | data formatting | bytes 65536

commit v7 on v6

--- a/solution.py
+++ b/solution.py
@@ -259,18 +259,25 @@
 
         def solve_second(after_y, finish):
             y0 = f0.at[1]
-            for side, held_by in ((quick, near), (slow, far)):
-                take(f1, h2, q2, side, 2, held_by, 1, -1)
-                take(y0, h2, q2, side, 1, held_by, 0, 1)
-                for kind, half in HALVES.items():
-                    take(y0, h2, q2, side, kind, held_by, 0, -1, alive[0] if held_by is far else None, half)
-            after_y()
 
             def forward(j, t):
-                f1[tile(j), :] = alive[1] * (f1[tile(j), :] - t)
-
-            products([(mat_l, y0)], forward, masks)
-            products([(mat_p1, f1)], finish, masks)
+                early[tile(j), :] = alive[1] * (f1[tile(j), :] - t)
+
+            def run(turn, _):
+                @pl.when(turn == 1)
+                def _():
+                    for side, held_by in ((quick, near), (slow, far)):
+                        take(f1, h2, q2, side, 2, held_by, 1, -1)
+                        take(y0, h2, q2, side, 1, held_by, 0, 1)
+                        for kind, half in HALVES.items():
+                            take(y0, h2, q2, side, kind, held_by, 0, -1, alive[0] if held_by is far else None, half)
+                    after_y()
+
+                products([(mat_l, y0)], forward, masks)
+                products([(mat_p1, early)], finish, masks)
+                return 0
+
+            lax.fori_loop(0, 2, run, 0)
 
         return own_part, far_first, solve_first, solve_second, alive, colours
 
@@ -313,17 +320,28 @@
         def result(j, t):
             out[0, tile(j), :] = jnp.where(colours == 1, alive[0] * t, cur0[tile(j), :])
 
-        up_early.wait_recv()
-        for part in PARTS:
-            landed(slow, part)
-            far_first(got_y.at[0], part)
-        again = []
-        for kind, half in HALVES.items():
-            begin = half.start // SUB
-            products([(mat_p0, got_y.at[0])], term, masks, begin, begin + half.size // SUB)
-            copies = again_copies(part_t, kind)
-            start_slow_first(copies)
-            again += copies
+        def run(turn, _):
+            @pl.when(turn == 1)
+            def _():
+                up_early.wait_recv()
+                f0[0] = got_y[0]
+                for part in PARTS:
+                    landed(slow, part)
+                    far_first(f0.at[0], part)
+
+            for kind, half in HALVES.items():
+                begin = half.start // SUB
+                products([(mat_p0, f0.at[0])], term, masks, begin, begin + half.size // SUB)
+
+                @pl.when(turn == 1)
+                def _():
+                    start_slow_first(again_copies(part_t, kind))
+
+            return 0
+
+        f0[0] = v0[...]
+        lax.fori_loop(0, 2, run, 0)
+        again = again_copies(part_t, 0) + again_copies(part_t, 3)
         down_t.start()
         for kind in HALVES:
             twin(part_t, kind, lambda c: c.start())

time: 19.8 us -> 19.9 us (level)
  no operation moved by 1% of the time
where the time goes in v7:
time: 19.9 us; the launch traced here: 19.8 us
  Pallas kernels  19.2 us (96%)
  local copies, waits for them, and re-layouts  0.62 us (3%)
    pallas_call x1, Pallas kernels, shards(): pl.pallas_call(functools.partial(kernel, groups), out_shape=pltpu.VMEM((1...  19.2 us
    unnamed x1, local copies, waits for them, and re-layouts  0.62 us

profile of v7, /device:TPU:1, one launch (start us, length us, event | category | flops | bytes accessed | tf_op | source)
XLA Modules:
  0.0 19.8 jit_solution(16182560524667510528)
XLA Ops:
  0.0 19.2 %shard_map.91 = f32[1,64,128]{2,1,0:T(8,128)S(1)} custom-call(f32[1,64,128]{2,1,0:T(8,128)} %rhs.1, f32[1,64,128]{2,1,0:T(8,128)} %prev.1, f32[1,64,64,128]{3,2,1,0:T(8,128)} %lower.1, f32[1,64,64,128]{3,2,1,0:T(8,128)} %pivot.1, f32[1,64,64,128]{3,2,1,0:T(8,128)} %upper.1, f32[4,1,64,128]{3,2,1,0:T(8,128)} %coupling.1, s32[4,128]{1,0:T(4,128)} %neighbours.1, ...), custom_call_target="tpu_custom_call" | custom-call | tf_op jit(solution)/shard_map/pallas_call | solution.py:555
  19.2 0.6 %copy.11 = f32[1,64,128]{2,1,0:T(8,128)} copy(f32[1,64,128]{2,1,0:T(8,128)S(1)} %shard_map.91) | data formatting | bytes 65536

commit v8 on v7

--- a/solution.py
+++ b/solution.py
@@ -118,9 +118,13 @@
     up_cur = wall_copy(cur1, cur1, 9, 0)
     up_early = wall_copy(early, got_y.at[0], 10, 0)
     up_y = wall_copy(f0.at[1], got_y.at[1], 11, 0)
-    up_far = {part: pltpu.make_async_remote_copy(
-        src_ref=piece(h1.at[slow, 0], part), dst_ref=piece(h1.at[slow, 0], part), send_sem=wsend.at[14 + part // 2],
-        recv_sem=q1.at[slow, part], device_id=(s, 0), device_id_type=MESH) for part in PARTS}
+    def up_raw(side, first_sem):
+        return {part: pltpu.make_async_remote_copy(
+            src_ref=piece(h1.at[side, 0], part), dst_ref=piece(h1.at[side, 0], part), send_sem=wsend.at[first_sem + part // 2],
+            recv_sem=q1.at[side, part], device_id=(s, 0), device_id_type=MESH) for part in PARTS}
+
+    up_far = up_raw(slow, 14)
+    up_near = up_raw(quick, 16)
     up_x = [wall_copy(x1.at[i], got_x.at[i], 12 + i, 0) for i in (0, 1)]
 
     def start_slow_first(copies):
@@ -232,16 +236,20 @@
             count = TILES if part == 1 else PARTS[part].size // SUB
             lax.fori_loop(begin, begin + count, body, 0, unroll=count)
 
+        def near_first(total, part):
+            take_first(total, quick, near, part)
+
         def far_first(total, part):
             take_first(total, slow, far, part, alive[0])
 
         def solve_first(finish):
             y0 = f0.at[0]
+            early[...] = y0[...]
+            up_early.start()
             for part in PARTS:
                 landed(quick, part)
+                up_near[part].start()
                 take_first(y0, quick, near, part)
-            early[...] = y0[...]
-            up_early.start()
             landed(quick, 1)
             take_first(f1, quick, near, 1)
             for part in PARTS:
@@ -279,7 +287,7 @@
 
             lax.fori_loop(0, 2, run, 0)
 
-        return own_part, far_first, solve_first, solve_second, alive, colours
+        return own_part, near_first, far_first, solve_first, solve_second, alive, colours
 
     @pl.when(w == 0)
     def _():
@@ -306,7 +314,7 @@
 
         for c in mine:
             c.wait()
-        own_part, far_first, solve_first, solve_second, alive, colours = make_solver()
+        own_part, near_first, far_first, solve_first, solve_second, alive, colours = make_solver()
 
         def term(j, t):
             part_t[tile(j), :] = jnp.where(colours == 0, alive[0] * t, v0[tile(j), :])
@@ -325,6 +333,9 @@
             def _():
                 up_early.wait_recv()
                 f0[0] = got_y[0]
+                for part in PARTS:
+                    landed(quick, part)
+                    near_first(f0.at[0], part)
                 for part in PARTS:
                     landed(slow, part)
                     far_first(f0.at[0], part)
@@ -450,7 +461,7 @@
 
         for c in mine[:6]:
             c.wait()
-        own_part, far_first, solve_first, solve_second, alive, colours = make_solver()
+        own_part, near_first, far_first, solve_first, solve_second, alive, colours = make_solver()
         own_part(f1, r1, 1, v1)
         for c in down[:3]:
             c.wait_recv()
@@ -505,7 +516,7 @@
 
         twin(cur1, 2, lambda c: c.wait_send())
         twin(part_u, 1, lambda c: c.wait_send())
-        finish_sends(first, [up_early, up_far[0], up_far[2], up_x[0]] + again0 + again1)
+        finish_sends(first, [up_early, up_near[0], up_near[2], up_far[0], up_far[2], up_x[0]] + again0 + again1)
 
         @pl.when(s == 0)
         def _():
@@ -561,7 +572,7 @@
         + [pltpu.VMEM((FACES, LANES), jnp.int32), line, line]
         + [pltpu.VMEM((2, 2, BLOCK, LANES), jnp.float32), pltpu.VMEM((2, 3, BLOCK, LANES), jnp.float32), pair]
         + [plane, pair] + [plane] * 5 + [pair] * 3
-        + [dma((8,)), dma((16,)), dma((14,)), dma((2, 3)), dma((2, 3)), dma((4, 2, 2)), dma((2, 4)), dma((3,)), dma((3,))]
+        + [dma((8,)), dma((18,)), dma((14,)), dma((2, 3)), dma((2, 3)), dma((4, 2, 2)), dma((2, 4)), dma((3,)), dma((3,))]
         + [pltpu.SemaphoreType.REGULAR((2,))],
         compiler_params=pltpu.CompilerParams(collective_id=0, has_side_effects=True, vmem_limit_bytes=16 << 20),
     )(*[pltpu.with_memory_space_constraint(a, pltpu.HBM) for a in here])

time: 19.9 us -> 19.9 us (level)
  no operation moved by 1% of the time
where the time goes in v8:
time: 19.9 us; the launch traced here: 19.8 us
  Pallas kernels  19.2 us (96%)
  local copies, waits for them, and re-layouts  0.62 us (3%)
    pallas_call x1, Pallas kernels, shards(): pl.pallas_call(functools.partial(kernel, groups), out_shape=pltpu.VMEM((1...  19.2 us
    unnamed x1, local copies, waits for them, and re-layouts  0.62 us

profile of v8, /device:TPU:1, one launch (start us, length us, event | category | flops | bytes accessed | tf_op | source)
XLA Modules:
  0.0 19.8 jit_solution(2538948901783786744)
XLA Ops:
  0.0 19.2 %shard_map.91 = f32[1,64,128]{2,1,0:T(8,128)S(1)} custom-call(f32[1,64,128]{2,1,0:T(8,128)} %rhs.1, f32[1,64,128]{2,1,0:T(8,128)} %prev.1, f32[1,64,64,128]{3,2,1,0:T(8,128)} %lower.1, f32[1,64,64,128]{3,2,1,0:T(8,128)} %pivot.1, f32[1,64,64,128]{3,2,1,0:T(8,128)} %upper.1, f32[4,1,64,128]{3,2,1,0:T(8,128)} %coupling.1, s32[4,128]{1,0:T(4,128)} %neighbours.1, ...), custom_call_target="tpu_custom_call" | custom-call | tf_op jit(solution)/shard_map/pallas_call | solution.py:566
  19.2 0.6 %copy.11 = f32[1,64,128]{2,1,0:T(8,128)} copy(f32[1,64,128]{2,1,0:T(8,128)S(1)} %shard_map.91) | data formatting | bytes 65536
